TPU v7x, 128 devices: a whole 4x4x4 slice. The times are simulated.
128 devices in a mesh: wide: 32 (over z, y, core), narrow: 4 (over x).
Axes of the slice: x: 4, y: 4, z: 4, core: 2. Of those that a mesh axis runs over, the one named last changes fastest.
Arguments:
- factors: bfloat16 [15, 7168, 1920], P(None, ('wide', 'narrow')), may hold values from -0.625 to 0.625
- t2_window: bfloat16 [16, 15, 15], replicated, may hold values from -0.3984375 to 0.3984375
- residual_in: bfloat16 [256, 16, 16384], P('wide', 'narrow'), may hold values from -6 to 6
- tile_mask: int32 [225], replicated, may hold values from 0 to 1, as said below
- owner_slot: int32 [225], replicated, may hold values from 0 to 63, as said below
- home_slot: int32 [225], replicated, may hold values from 0 to 255, as said below
Outputs:
- residual_out: bfloat16 [256, 16, 16384], P('wide', 'narrow')
- ladder_norms: float32 [64, 16], P('wide', 'narrow')
Inputs may be any that keep to these rules, and one draw needn't show every extreme that they name: `tile_mask`: exactly 64 tiles are filled. `owner_slot`: the filled tiles take the owner slots 0 to 63, one each; slot o belongs to wide index o // 2; the filled tiles of one wide index have different home wide indices. Entries of tiles that are not filled mean nothing. `home_slot`: all different; home slot s lies on wide index s // 8.
All inputs are finite; a program needn't handle non-finite values.
Results may differ from a plain program's by a relative error of at most 0.0045.
Values may be sent and summed in bfloat16 or wider, within the bound.
A program may use at most 192 MiB of HBM per device.

v0:
```python
import jax
import jax.numpy as jnp
from jax import lax
from jax.sharding import PartitionSpec as P

SLOTS = 2


def tile_contract(first_side, second_side, amplitude, window):
    precise = lax.Precision.HIGHEST
    tile_width = first_side.shape[1] // window
    integral = lax.dot_general(
        first_side, second_side, (((0,), (0,)), ((), ())), preferred_element_type=jnp.float32
    )
    accumulated = jnp.einsum(
        "cadb,pcd->pab",
        integral.reshape(window, tile_width, window, tile_width),
        amplitude,
        precision=precise,
    )
    return accumulated.reshape(amplitude.shape[0], tile_width * tile_width)


def body(factors, t2_window, residual_in, tile_mask, owner_slot, home_slot):
    owner_count = lax.axis_size("wide")
    clusters = factors.shape[0]
    window = t2_window.shape[1]
    amplitude = t2_window.astype(jnp.float32)
    filled_total = owner_count * SLOTS
    tile_ids = jnp.arange(tile_mask.shape[0], dtype=jnp.int32)
    is_filled = tile_mask == 1
    owner_match = is_filled[:, None] & (
        owner_slot[:, None] == jnp.arange(filled_total, dtype=jnp.int32)[None, :]
    )
    tile_of_slot = jnp.sum(jnp.where(owner_match, tile_ids[:, None], 0), axis=0)
    slot_pairs = tile_of_slot.reshape(owner_count, SLOTS)
    cluster_ids = jnp.stack([slot_pairs // clusters, slot_pairs % clusters], axis=2)
    outgoing = jnp.take(factors, cluster_ids, axis=0)
    received = lax.all_to_all(outgoing, "wide", split_axis=0, concat_axis=0, tiled=True)
    aux_rows = received.shape[0] * received.shape[3]

    def one_tile(position):
        slot_blocks = lax.dynamic_index_in_dim(received, position, 1, keepdims=False)
        first_side = slot_blocks[:, 0].reshape(aux_rows, slot_blocks.shape[-1])
        second_side = slot_blocks[:, 1].reshape(aux_rows, slot_blocks.shape[-1])
        return tile_contract(first_side, second_side, amplitude, window)

    partial_terms = lax.map(one_tile, jnp.arange(received.shape[1], dtype=jnp.int32))
    ladder = lax.psum_scatter(partial_terms, "narrow", scatter_dimension=1, tiled=True).astype(
        jnp.bfloat16
    )
    ladder_wide = ladder.astype(jnp.float32)
    ladder_norms = jnp.mean(ladder_wide * ladder_wide, axis=2)
    home_count = residual_in.shape[0]
    home_ids = lax.axis_index("wide") * home_count + jnp.arange(home_count, dtype=jnp.int32)
    present = is_filled[:, None] & (home_slot[:, None] == home_ids[None, :])
    kept_slot = jnp.any(present, axis=0)
    source_slot = jnp.sum(jnp.where(present, owner_slot[:, None], 0), axis=0)
    gathered_rows = lax.all_gather(ladder, "wide", axis=0, tiled=True)
    owner_rows = jnp.arange(gathered_rows.shape[0], dtype=jnp.int32)
    pick_matrix = (source_slot[:, None] == owner_rows[None, :]) & kept_slot[:, None]
    home_ladder = jnp.einsum(
        "jm,mpx->jpx",
        pick_matrix.astype(jnp.bfloat16),
        gathered_rows,
        preferred_element_type=jnp.float32,
    )
    combined = residual_in.astype(jnp.float32) + home_ladder
    residual_out = jnp.where(kept_slot[:, None, None], combined, 0.0).astype(jnp.bfloat16)
    return (residual_out, ladder_norms)


def solution(mesh):
    in_specs = (P(None, ("wide", "narrow"), None), P(), P("wide", "narrow", None), P(), P(), P())
    out_specs = (P("wide", "narrow", None), P("wide", "narrow"))
    return jax.shard_map(body, mesh=mesh, in_specs=in_specs, out_specs=out_specs, check_vma=False)
```

profile of v0, /device:TPU:1, one launch (start us, length us, event | category | flops | bytes accessed | tf_op | source)
XLA Modules:
  0.0 737.5 jit_solution(7786348903344628361)
XLA Ops:
  7.2 0.0 copy-start
  7.2 0.8 broadcast_compare_fusion.1
  8.0 0.9 select_reduce_fusion
  9.0 0.1 div.32
  9.1 0.1 rem.54
  9.2 0.1 ne.100
  9.3 0.1 copy.60
  9.4 0.1 copy.57
  9.5 0.1 copy.61
  9.6 0.1 copy.58
  9.7 0.1 copy.62
  9.8 0.2 reshape.193
  10.0 0.1 copy.59
  10.1 12.0 %gather_fusion = bf16[128,56,1920]{2,1,0:T(8,128)(2,1)} fusion(bf16[15,56,1920]{2,1,0:T(8,128)(2,1)S(1)} %copy-done, s32[1024]{0:T(1024)S(1)} %pad_clamp_fusion), kind=kCustom, calls=%fused_computation | custom fusion | bytes 55050752 | tf_op jit(solution)/shard_map/jit(_take)/gather | solution.py:38
  22.1 19.3 %broadcast_select_fusion = bf16[32,2,2,56,1920]{4,3,2,1,0:T(8,128)(2,1)} fusion(bf16[32,2,2,56,1920]{4,3,2,1,0:T(8,128)(2,1)} %bitcast.63, pred[32,2,2]{2,1,0:T(4,128)(4,1)S(1)} %copy.59), kind=kLoop, calls=%fused_computation.7 | loop fusion | flops 13762560 | bytes 55050368 | tf_op jit(solution)/shard_map/jit(_take)/select_n | solution.py:38
  41.4 9.8 %all-to-all-start = ((bf16[32,2,2,56,1920]{4,3,2,1,0:T(8,128)(2,1)}), bf16[32,2,2,56,1920]{4,3,2,1,0:T(8,128)(2,1)}, u32[]{:S(2)}, u32[]{:S(2)}) async-start(bf16[32,2,2,56,1920]{4,3,2,1,0:T(8,128)(2,1)} %broadcast_select_fusion), calls=%async_computation | async-start | bytes 55050240 | tf_op jit(solution)/shard_map/all_to_all | solution.py:39
  51.2 0.0 all-gather.2.cloned.1.call-start
  51.3 0.6 dynamic-slice
  52.6 335.8 %all-to-all-done = bf16[32,2,2,56,1920]{4,3,2,1,0:T(8,128)(2,1)} async-done(((bf16[32,2,2,56,1920]{4,3,2,1,0:T(8,128)(2,1)}), bf16[32,2,2,56,1920]{4,3,2,1,0:T(8,128)(2,1)}, u32[]{:S(2)}, u32[]{:S(2)}) %all-to-all-start) | async-done | bytes 27525152 | tf_op jit(solution)/shard_map/all_to_all | solution.py:39
  388.3 215.2 %while.10 = (s32[]{:T(128)}, f32[2,16,16384]{2,0,1:T(2,128)}, s32[2]{0:T(128)S(1)}, bf16[32,2,2,56,1920]{4,3,2,1,0:T(8,128)(2,1)}, f32[16,15,15]{2,0,1:T(8,128)S(1)}, /*index=5*/s32[]{:T(128)}, s32[]{:T(128)}, s32[]{:T(128)}) while((s32[]{:T(128)}, f32[2,16,16384]{2,0,1:T(2,128)}, s32[2]{0:T(128)S(1)}, ...), condition=%wide.region_4.5_spmd, body=%wide.region_3.4_spmd.sunk | while | flops 13919846400 | bytes 131086536 | solution.py:48
  405.0 0.6 dynamic_slice.13
  407.5 7.2 copy_bitcast_fusion.2
  414.7 5.4 fusion.31
  420.2 9.9 %copy.90 = bf16[1920,1792]{1,0:T(8,128)(2,1)} copy(bf16[1920,1792]{0,1:T(8,128)(2,1)} %bitcast.60) | data formatting | bytes 13762560 | tf_op jit(solution)/shard_map/while/body/eval_jaxpr/dot_general | solution.py:12
  430.1 9.8 %copy.91 = bf16[1920,1792]{1,0:T(8,128)(2,1)} copy(bf16[1920,1792]{0,1:T(8,128)(2,1)} %bitcast.59) | data formatting | bytes 13762560 | tf_op jit(solution)/shard_map/while/body/eval_jaxpr/dot_general | solution.py:12
  439.9 20.6 %fusion.32 = f32[15,128,15,128]{3,1,2,0:T(8,128)S(1)} fusion(bf16[15,128,1792,1]{2,1,3,0:T(8,128)(2,1)} %bitcast.61, bf16[15,128,1792,1]{2,1,0,3:T(8,128)(2,1)} %bitcast.62), kind=kOutput, calls=%fused_computation.39.clone.1 | convolution fusion | flops 13212057600 | bytes 28508160 | tf_op jit(solution)/shard_map/while/body/eval_jaxpr/dot_general | solution.py:12
  460.5 20.3 %fusion.33 = f32[16,128,128]{2,0,1:T(8,128)S(1)} fusion(f32[15,128,15,128]{3,1,2,0:T(8,128)S(1)} %fusion.32, f32[16,15,15]{2,0,1:T(8,128)S(1)} %get-tuple-element.128), kind=kOutput, calls=%fused_computation.4.clone.1 | convolution fusion | flops 707788800 | bytes 15808576 | tf_op jit(solution)/shard_map/while/body/eval_jaxpr/cadb,pcd->pab/dot_general | solution.py:15
  480.9 0.3 copy.92
  481.2 18.5 %dynamic_update_slice.5 = f32[2,16,16384]{2,0,1:T(2,128)} dynamic-update-slice(f32[2,16,16384]{2,0,1:T(2,128)} %get-tuple-element.117, f32[1,16,16384]{2,0,1:T(1,128)S(1)} %bitcast.64, s32[]{:T(128)} %get-tuple-element.116, s32[]{:T(128)} %constant.57.clone.1..sunk, s32[]{:T(128)} %constant.57.clone.1..sunk) | dynamic-update-slice | bytes 2097156 | tf_op jit(solution)/shard_map/while/body/jit(dynamic_update_index_in_dim)/dynamic_update_slice | solution.py:48
  499.7 0.6 dynamic_slice.13
  502.3 7.2 copy_bitcast_fusion.2
  509.5 5.4 fusion.31
  514.9 9.9 %copy.90 = bf16[1920,1792]{1,0:T(8,128)(2,1)} copy(bf16[1920,1792]{0,1:T(8,128)(2,1)} %bitcast.60) | data formatting | bytes 13762560 | tf_op jit(solution)/shard_map/while/body/eval_jaxpr/dot_general | solution.py:12
  524.8 9.8 %copy.91 = bf16[1920,1792]{1,0:T(8,128)(2,1)} copy(bf16[1920,1792]{0,1:T(8,128)(2,1)} %bitcast.59) | data formatting | bytes 13762560 | tf_op jit(solution)/shard_map/while/body/eval_jaxpr/dot_general | solution.py:12
  534.7 20.6 %fusion.32 = f32[15,128,15,128]{3,1,2,0:T(8,128)S(1)} fusion(bf16[15,128,1792,1]{2,1,3,0:T(8,128)(2,1)} %bitcast.61, bf16[15,128,1792,1]{2,1,0,3:T(8,128)(2,1)} %bitcast.62), kind=kOutput, calls=%fused_computation.39.clone.1 | convolution fusion | flops 13212057600 | bytes 28508160 | tf_op jit(solution)/shard_map/while/body/eval_jaxpr/dot_general | solution.py:12
  555.3 20.3 %fusion.33 = f32[16,128,128]{2,0,1:T(8,128)S(1)} fusion(f32[15,128,15,128]{3,1,2,0:T(8,128)S(1)} %fusion.32, f32[16,15,15]{2,0,1:T(8,128)S(1)} %get-tuple-element.128), kind=kOutput, calls=%fused_computation.4.clone.1 | convolution fusion | flops 707788800 | bytes 15808576 | tf_op jit(solution)/shard_map/while/body/eval_jaxpr/cadb,pcd->pab/dot_general | solution.py:15
  575.6 0.3 copy.92
  575.9 18.5 %dynamic_update_slice.5 = f32[2,16,16384]{2,0,1:T(2,128)} dynamic-update-slice(f32[2,16,16384]{2,0,1:T(2,128)} %get-tuple-element.117, f32[1,16,16384]{2,0,1:T(1,128)S(1)} %bitcast.64, s32[]{:T(128)} %get-tuple-element.116, s32[]{:T(128)} %constant.57.clone.1..sunk, s32[]{:T(128)} %constant.57.clone.1..sunk) | dynamic-update-slice | bytes 2097156 | tf_op jit(solution)/shard_map/while/body/jit(dynamic_update_index_in_dim)/dynamic_update_slice | solution.py:48
  603.5 29.3 %all-reduce.2 = bf16[2,16,16384]{2,0,1:T(2,128)(2,1)S(1)} all-reduce(f32[2,16,16384]{2,0,1:T(2,128)} %get-tuple-element.29), channel_id=2, replica_groups=mesh['wide'=32,'narrow'=4] {'narrow'}, use_global_device_ids=true, to_apply=%region_5.6.clone | all-reduce | flops 524288 | bytes 3145728
  632.8 0.5 multiply_reduce_fusion
  633.3 0.9 copy.65
  634.2 0.0 all-gather.2.cloned.1.call-update
  634.2 0.2 fusion.10
  634.4 0.2 select_reduce_fusion.1
  634.6 0.6 copy.68
  635.3 79.8 %all-gather.2.cloned.1.call-done = bf16[64,4,16384]{2,1,0:T(4,128)(2,1)} async-done(((bf16[2,4,16384]{2,1,0:T(4,128)(2,1)}), bf16[64,4,16384]{2,1,0:T(4,128)(2,1)}) %all-gather.2.cloned.1.call-update) | async-done | bytes 8388624 | tf_op jit(solution)/shard_map/all_gather | solution.py:59
  715.1 13.5 %fusion.7 = bf16[8,4,16384]{2,0,1:T(8,128)(2,1)S(1)} fusion(bf16[64,4,16384]{2,1,0:T(4,128)(2,1)} %all-gather.2.cloned.1.call-done, bf16[8,4,16384]{2,1,0:T(4,128)(2,1)} %param.10, pred[8]{0:T(512)(128)(4,1)S(1)} %fusion.10, s32[8]{0:T(128)S(1)} %select_reduce_fusion.1), kind=kOutput, calls=%fused_computation.10 | convolution fusion | flops 69207040 | bytes 10485800 | tf_op jit(solution)/shard_map/jm,mpx->jpx/dot_general | solution.py:62
  728.6 1.8 copy.67
  (26 shorter events, 0.1 us)
Async XLA Ops:
  7.2 2.9 copy-start
  8.0 1.0 copy-start.3
  41.4 9.9 %copy-start.2 = (bf16[16,15,15]{2,0,1:T(8,128)(2,1)S(1)}, bf16[16,15,15]{2,0,1:T(8,128)(2,1)}, u32[]{:S(2)}) copy-start(bf16[16,15,15]{2,0,1:T(8,128)(2,1)} %param.9) | copy-start | bytes 21604
  41.4 9.9 %copy-start.7 = (u32[128]{0:T(128)S(1)}, u32[128]{0:T(128)}, u32[]{:S(2)}) copy-start(u32[128]{0:T(128)} %constant.68) | copy-start | bytes 1540
  41.4 346.9 %all-to-all-start = ((bf16[32,2,2,56,1920]{4,3,2,1,0:T(8,128)(2,1)}), bf16[32,2,2,56,1920]{4,3,2,1,0:T(8,128)(2,1)}, u32[]{:S(2)}, u32[]{:S(2)}) async-start(bf16[32,2,2,56,1920]{4,3,2,1,0:T(8,128)(2,1)} %broadcast_select_fusion), calls=%async_computation | async-start | bytes 55050240 | tf_op jit(solution)/shard_map/all_to_all | solution.py:39
  51.2 663.9 %all-gather.2.cloned.1.call-start = ((), (), s32[]{:S(2)}) async-start(), calls=%async_computation.1 | async-start | bytes 8650752 | tf_op jit(solution)/shard_map/all_gather | solution.py:59
  388.3 245.9 %copy-start.4 = (pred[225]{0:T(512)(128)(4,1)S(1)}, pred[225]{0:T(512)(128)(4,1)}, u32[]{:S(2)}) copy-start(pred[225]{0:T(512)(128)(4,1)} %copy-done.3) | copy-start | bytes 679
  388.3 245.9 %copy-start.6 = (s32[225]{0:T(256)S(1)}, s32[225]{0:T(256)}, u32[]{:S(2)}) copy-start(s32[225]{0:T(256)} %param.13) | copy-start | bytes 2704
  388.3 246.1 %copy-start.5 = (s32[225]{0:T(256)S(1)}, s32[225]{0:T(256)}, u32[]{:S(2)}) copy-start(s32[225]{0:T(256)} %param.12) | copy-start | bytes 2704
  634.6 95.8 %copy-start.1 = (bf16[15,56,1920]{2,1,0:T(8,128)(2,1)S(1)}, bf16[15,56,1920]{2,1,0:T(8,128)(2,1)}, u32[]{:S(2)}) copy-start(bf16[15,56,1920]{2,1,0:T(8,128)(2,1)} %param.8) | copy-start | bytes 9676804
Sparse Core Ops, SparseCore 0:
  634.3 80.7 all-gather.1
where the time goes:
time: 744 us; the launch traced here: 737 us
  waiting for transfers between devices  416 us (56%)
  local copies, waits for them, and re-layouts  121 us (16%)
  matrix products  95.4 us (13%)
  loops' own time  29.6 us (4%)
  blocking collectives  29.3 us (4%)
  other arithmetic  22 us (3%)
  between operations  15.1 us (2%)
  starting transfers between devices  9.84 us (1%)
    all_to_all x1, waiting for transfers between devices, body(): lax.all_to_all(outgoing, 'wide', split_axis=0, concat_axis=0, tiled=True)  336 us
    all_gather x1, waiting for transfers between devices, body(): gathered_rows = lax.all_gather(ladder, 'wide', axis=0, tiled=True)  79.8 us
    dot_general x2, matrix products, tile_contract(): lax.dot_general(first_side, second_side, (((0,), (0,)), ((), ())), prefer...  41.2 us
    dot_general x2, matrix products, tile_contract(): jnp.einsum('cadb,pcd->pab', integral.reshape(window, tile_width, window,...  40.7 us
    dot_general x4, local copies, waits for them, and re-layouts, tile_contract(): lax.dot_general(first_side, second_side, (((0,), (0,)), ((), ())), prefer...  39.6 us
    dynamic_update_slice x2, local copies, waits for them, and re-layouts, body(): lax.map(one_tile, jnp.arange(received.shape[1], dtype=jnp.int32))  37 us
    another operation x1, loops' own time, body(): lax.map(one_tile, jnp.arange(received.shape[1], dtype=jnp.int32))  29.6 us
    unnamed x1, blocking collectives  29.3 us
  transfers between devices with their start and end apart: 2, of which 2 were waited for; matrix products, arithmetic and copies ran while one was open for 0% of the time, Pallas kernels for 0%

commit v1 on v0

v1 whole, which is shorter than its diff:
```python
import functools

import jax
import jax.numpy as jnp
from jax import lax
from jax.experimental import pallas as pl
from jax.experimental.pallas import tpu as pltpu
from jax.sharding import PartitionSpec as P

BF = jnp.bfloat16
F32 = jnp.float32
MESH = pl.DeviceIdType.MESH
VT = 128
W = 15
NC = 15
ROWS = 56
KC = 1792
FILLED = 64


def place():
    w = lax.axis_index("wide")
    return lax.axis_index("narrow"), (w // 2) % 4, w // 8, w % 2


def at(x, y, z, c):
    return {"wide": z * 8 + y * 2 + c, "narrow": x}


def ladder_kernel(
    first, second, amp, own_rows,
    spread, other_rows,
    weights, f2, f1t, y_buf, out, raw, rx, ry, rz, r2, r3,
    ex_s, ex_r, ld_s, x_s, x_r, y_s, y_r, z_s, z_r, s2_s, s2_r, s3_s, s3_r, ag_s, ag_r, co_s, co_r, st_s,
):
    x, y, z, c = place()
    ring = {
        "x": (x, at((x + 1) % 4, y, z, c), at((x + 3) % 4, y, z, c)),
        "y": (y, at(x, (y + 1) % 4, z, c), at(x, (y + 3) % 4, z, c)),
        "z": (z, at(x, y, (z + 1) % 4, c), at(x, y, (z + 3) % 4, c)),
    }
    partner = at(x, y, z, 1 - c)

    barrier = pltpu.get_barrier_semaphore()
    greeted = [partner] + [ring[a][i] for a in "xyz" for i in (1, 2)]
    for device in greeted:
        pl.semaphore_signal(barrier, inc=1, device_id=device, device_id_type=MESH)
    pl.semaphore_wait(barrier, len(greeted))

    def remote(src, dst, s_sem, r_sem, device):
        return pltpu.make_async_remote_copy(
            src_ref=src, dst_ref=dst, send_sem=s_sem, recv_sem=r_sem, device_id=device, device_id_type=MESH
        )

    def exchange(i):
        return remote(own_rows.at[i], other_rows.at[i], ex_s.at[i], ex_r.at[i], partner)

    def start_exchange(i, _):
        exchange(i).start()
        return 0

    lax.fori_loop(0, NC, start_exchange, 0)

    row = lax.broadcasted_iota(jnp.int32, (256, 16), 0)
    col = lax.broadcasted_iota(jnp.int32, (256, 16), 1)
    widen = (row // 16 == col).astype(F32).astype(BF)
    row2 = lax.broadcasted_iota(jnp.int32, (256, 256), 0)
    col2 = lax.broadcasted_iota(jnp.int32, (256, 256), 1)
    same = row2 % 16 == col2 % 16
    for i in range(8):
        tall = jnp.dot(widen, amp[i], preferred_element_type=F32).astype(BF)
        full = lax.dot_general(tall, widen, (((1,), (1,)), ((), ())), preferred_element_type=F32)
        weights[i // 2, (i % 2) * 256:(i % 2) * 256 + 256, :] = jnp.where(same, full, 0.0).astype(BF)

    def load(which, i):
        src = (own_rows, other_rows)[which]
        return pltpu.make_async_copy(src.at[i], raw.at[which, i % 2], ld_s.at[which, i % 2])

    def start_load(i):
        load(0, i).start()
        exchange(i).wait_recv()
        load(1, i).start()

    start_load(0)
    f2[52, :, 128:256] = jnp.zeros((256, 128), BF)

    def assemble(i, _):
        @pl.when(i + 1 < NC)
        def _():
            start_load(i + 1)

        load(0, i).wait()
        load(1, i).wait()
        slot = i % 2
        for blk in range(7):
            parts = []
            for d in range(W):
                lanes = slice(d * 128, d * 128 + 128)
                if blk < 6:
                    r0 = (blk % 3) * 16
                    parts.append(raw[blk // 3, slot, r0:r0 + 16, lanes])
                else:
                    parts.append(
                        jnp.concatenate([raw[0, slot, 48:56, lanes], raw[1, slot, 48:56, lanes]], axis=0)
                    )
            parts.append(jnp.zeros((16, 128), BF))
            block = jnp.concatenate(parts, axis=0)
            f1t[i, :, blk * 256:blk * 256 + 256] = block.T
            if blk < 6:
                f2[i * 3 + blk // 2, :, (blk % 2) * 128:(blk % 2) * 128 + 128] = block
            else:
                f2[45 + i // 2, :, pl.ds(pl.multiple_of((i % 2) * 128, 128), 128)] = block
        return 0

    lax.fori_loop(0, NC, assemble, 0)

    def put(axis, view, recv, s_sem, r_sem, way, kind):
        step = 2 if kind == 0 else (1 if way == 0 else 3)
        half = {0: way, 1: 1 - way, 2: way}[kind]
        return remote(view(step, half), recv(way, kind), s_sem(way, kind), r_sem(way, kind), ring[axis][1 + way])

    def add_tiles(dst, terms, n):
        def one(i, _):
            total = dst.at[i][...].astype(F32)
            for term in terms:
                total = total + term.at[i][...].astype(F32)
            dst.at[i][...] = total.astype(BF)
            return 0

        lax.fori_loop(0, n, one, 0)

    def view1(axis, s):
        coord, base = ring[axis][0], 32 if axis == "y" else 48
        return lambda k, h: out.at[s, :, pl.ds(base + ((coord + k) % 4) * 4 + 2 * h, 2)]

    def put1(axis, s, way, kind):
        buf, ss, rs = (ry, y_s, y_r) if axis == "y" else (rz, z_s, z_r)
        return put(
            axis, view1(axis, s), lambda w, k: buf.at[w, k, s], lambda w, k: ss.at[s, w, k],
            lambda w, k: rs.at[s, w, k], way, kind,
        )

    def later1(axis, s):
        buf = ry if axis == "y" else rz
        for way in (0, 1):
            put1(axis, s, way, 0).wait_recv()
            dst = view1(axis, s)(1 if way == 0 else 3, way)
            for slot in range(2):
                add_tiles(dst.at[slot], [buf.at[way, 0, s, slot]], 2)
            put1(axis, s, way, 2).start()

    X_AT = {(0, 0): (0, 0), (1, 0): (0, 1), (0, 1): (1, 0), (1, 1): (1, 1), (0, 2): (2, 0), (1, 2): (2, 1)}

    def put_x(b, way, kind):
        s, slot = X_AT[(way, kind)]
        return remote(
            out.at[s, slot, b * 16:b * 16 + 16], rx.at[b, way, kind], x_s.at[b, way, kind], x_r.at[b, way, kind],
            ring["x"][1 + way],
        )

    def compute(s, b):
        def group(i, _):
            for u in range(8):
                t = b * 16 + i * 8 + u
                o = jnp.dot(f1t[first[t]], y_buf[second[t]], preferred_element_type=F32).astype(BF)
                out[s, 0, t] = o[:, :128]
                out[s, 1, t] = o[:, 128:]
            return 0

        lax.fori_loop(0, 2, group, 0)

    def amplitudes(s):
        def put_block(o, i, blk, half):
            rows = slice(blk * 256, blk * 256 + 256)
            for slot in range(2):
                y_buf[i, rows, slot * 128:slot * 128 + 128] = o[slot * 256:slot * 256 + 256, half * 128:half * 128 + 128]

        def cluster(i, _):
            for j in range(3):
                o = jnp.dot(weights[s], f2[i * 3 + j], preferred_element_type=F32).astype(BF)
                for half in range(2):
                    put_block(o, i, 2 * j + half, half)
            return 0

        lax.fori_loop(0, NC, cluster, 0)

        def tail(i, _):
            o = jnp.dot(weights[s], f2[45 + i], preferred_element_type=F32).astype(BF)
            for half in range(2):
                put_block(o, 2 * i + half, 6, half)
            return 0

        lax.fori_loop(0, 7, tail, 0)
        o = jnp.dot(weights[s], f2[52], preferred_element_type=F32).astype(BF)
        put_block(o, 14, 6, 0)

    def step(s, _):
        amplitudes(s)
        for b in (0, 1):
            compute(s, b)

            @pl.when(s == 0)
            def _():
                for way in (0, 1):
                    put_x(b, way, 0).start()

            @pl.when(s == 1)
            def _():
                for way in (0, 1):
                    put_x(b, way, 1).start()

            @pl.when(s == 2)
            def _():
                for way in (0, 1):
                    put_x(b, way, 0).wait_recv()
                    add_tiles(out.at[2, way, b * 16:b * 16 + 16], [rx.at[b, way, 0]], 16)
                    put_x(b, way, 2).start()

        for b, axis in ((2, "y"), (3, "z")):
            compute(s, b)
            for kind in (0, 1):
                for way in (0, 1):
                    put1(axis, s, way, kind).start()

            @pl.when(s >= 1)
            def _():
                later1(axis, s - 1)
        return 0

    lax.fori_loop(0, 4, step, 0)

    def stage(axis, view, recv, sems, n):
        def one(way, kind):
            return put(axis, view, recv, lambda w, k: sems[0].at[w, k], lambda w, k: sems[1].at[w, k], way, kind)

        for kind in (0, 1):
            for way in (0, 1):
                one(way, kind).start()
        yield
        for way in (0, 1):
            one(way, 0).wait_recv()
            add_tiles(view(1 if way == 0 else 3, way), [recv(way, 0)], n)
            one(way, 2).start()
        yield
        for kind in (1, 2):
            for way in (0, 1):
                one(way, kind).wait_recv()
        add_tiles(view(0, 0), [recv(0, 2), recv(1, 1)], n)
        add_tiles(view(0, 1), [recv(0, 1), recv(1, 2)], n)

    mine = pl.ds(2 * c, 2)

    def gather(axis, block, own, sems):
        def copy(i):
            way = i % 2
            if i < 2:
                src = own
                dst = spread.at[mine, block(0)]
            else:
                k = 3 if way == 0 else 1
                src = spread.at[2 * c + way, block(k)]
                dst = src
            return remote(src, dst, sems[0].at[i], sems[1].at[i], ring[axis][1 + way])

        copy(0).start()
        copy(1).start()
        yield
        copy(0).wait_recv()
        copy(2).start()
        copy(1).wait_recv()
        copy(3).start()
        yield
        copy(2).wait_recv()
        copy(3).wait_recv()

    def batch(b):
        base = 16 * b
        major = "y" if b in (0, 2) else "z"
        minor = "z" if major == "y" else "y"
        hi, lo = ring[major][0], ring[minor][0]
        if b < 2:
            for way in (0, 1):
                for kind in (1, 2):
                    put_x(b, way, kind).wait_recv()
            add_tiles(out.at[3, 0, base:base + 16], [rx.at[b, 0, 2], rx.at[b, 1, 1]], 16)
            add_tiles(out.at[3, 1, base:base + 16], [rx.at[b, 0, 1], rx.at[b, 1, 2]], 16)
            yield
            yield from stage(
                major, lambda k, h: out.at[3, h, pl.ds(base + ((hi + k) % 4) * 4, 4)],
                lambda w, k: r2.at[b, w, k], (s2_s.at[b], s2_r.at[b]), 4,
            )
            yield
            yield from stage(
                minor, lambda k, h: out.at[3, h, pl.ds(base + hi * 4 + (lo + k) % 4, 1)],
                lambda w, k: r3.at[b, w, k], (s3_s.at[b], s3_r.at[b]), 1,
            )
        else:
            buf = ry if b == 2 else rz
            later1(major, 3)
            yield
            for s in range(4):
                for way in (0, 1):
                    for kind in (1, 2):
                        put1(major, s, way, kind).wait_recv()
                for slot in range(2):
                    own = lambda h: out.at[s, slot, pl.ds(base + hi * 4 + 2 * h, 2)]
                    add_tiles(own(0), [buf.at[0, 2, s, slot], buf.at[1, 1, s, slot]], 2)
                    add_tiles(own(1), [buf.at[0, 1, s, slot], buf.at[1, 2, s, slot]], 2)
            yield
            yield from stage(
                minor, lambda k, h: out.at[:, h, base + hi * 4 + (lo + k) % 4],
                lambda w, k: r2.at[b, w, k], (s2_s.at[b], s2_r.at[b]), 4,
            )
            yield
            tile = pl.ds(base + hi * 4 + lo, 1)

            def plane(k, h):
                s, slot = {(2, 0): (0, 0), (2, 1): (0, 1), (1, 1): (1, 0), (3, 0): (1, 1), (1, 0): (2, 0),
                           (3, 1): (2, 1), (0, 0): (3, 0), (0, 1): (3, 1)}[(k, h)]
                return out.at[s, slot, tile]

            yield from stage(
                "x", plane, lambda w, k: r3.at[b, w, k], (s3_s.at[b], s3_r.at[b]), 1,
            )
        tile = pl.ds(base + hi * 4 + lo, 1)
        final = out.at[3, :, tile]
        keep = pltpu.make_async_copy(final, spread.at[mine, tile], st_s.at[b])
        keep.start()
        yield
        yield from gather(
            minor, lambda k: pl.ds(base + hi * 4 + (lo + k) % 4, 1), final, (ag_s.at[b, 0], ag_r.at[b, 0])
        )
        keep.wait()
        yield
        group = pl.ds(base + hi * 4, 4)
        yield from gather(
            major, lambda k: pl.ds(base + ((hi + k) % 4) * 4, 4), spread.at[mine, group],
            (ag_s.at[b, 1], ag_r.at[b, 1]),
        )
        core_copy(b).start()

    def core_copy(b):
        rows = spread.at[mine, pl.ds(16 * b, 16)]
        return remote(rows, rows, co_s.at[b], co_r.at[b], partner)

    chains = [batch(b) for b in (2, 3, 0, 1)]
    while chains:
        for chain in list(chains):
            try:
                next(chain)
            except StopIteration:
                chains.remove(chain)
    for b in range(4):
        core_copy(b).wait_recv()

    def wait_exchange(i, _):
        exchange(i).wait_send()
        return 0

    lax.fori_loop(0, NC, wait_exchange, 0)
    for b in range(2):
        for way in (0, 1):
            for kind in range(3):
                put_x(b, way, kind).wait_send()

    def wait1(s, _):
        for axis in "yz":
            for way in (0, 1):
                for kind in range(3):
                    put1(axis, s, way, kind).wait_send()
        return 0

    lax.fori_loop(0, 4, wait1, 0)
    for b in range(4):
        for way in (0, 1):
            for kind in range(3):
                remote(r2.at[b, way, kind], r2.at[b, way, kind], s2_s.at[b, way, kind], s2_r.at[b, way, kind],
                       partner).wait_send()
                remote(r3.at[b, way, kind], r3.at[b, way, kind], s3_s.at[b, way, kind], s3_r.at[b, way, kind],
                       partner).wait_send()
        for stage_no, n in ((0, 1), (1, 4)):
            for i in range(4):
                part = spread.at[pl.ds(0, 2), pl.ds(0, n)] if i < 2 else spread.at[0, pl.ds(0, n)]
                remote(part, part, ag_s.at[b, stage_no, i], ag_r.at[b, stage_no, i], partner).wait_send()
        core_copy(b).wait_send()


def ladders(first, second, amp, factors):
    dma = pltpu.SemaphoreType.DMA
    any_space = pl.BlockSpec(memory_space=pl.ANY)
    smem = pl.BlockSpec(memory_space=pltpu.SMEM)
    vmem = pl.BlockSpec(memory_space=pltpu.VMEM)
    flops = 2 * FILLED * 8 * VT * VT * KC
    spread, _ = pl.pallas_call(
        ladder_kernel,
        out_shape=(
            jax.ShapeDtypeStruct((4, FILLED, VT, VT), BF),
            jax.ShapeDtypeStruct(factors.shape, BF),
        ),
        in_specs=[smem, smem, vmem, any_space],
        out_specs=(any_space, any_space),
        scratch_shapes=[
            pltpu.VMEM((4, 512, 256), BF),
            pltpu.VMEM((53, 256, 256), BF),
            pltpu.VMEM((NC, VT, KC), BF),
            pltpu.VMEM((NC, KC, 256), BF),
            pltpu.VMEM((4, 2, FILLED, VT, VT), BF),
            pltpu.VMEM((2, 2, ROWS, W * VT), BF),
            pltpu.VMEM((2, 2, 3, 16, VT, VT), BF),
            pltpu.VMEM((2, 3, 4, 2, 2, VT, VT), BF),
            pltpu.VMEM((2, 3, 4, 2, 2, VT, VT), BF),
            pltpu.VMEM((4, 2, 3, 4, VT, VT), BF),
            pltpu.VMEM((4, 2, 3, 1, VT, VT), BF),
            dma((NC,)), dma((NC,)), dma((2, 2)),
            dma((2, 2, 3)), dma((2, 2, 3)),
            dma((4, 2, 3)), dma((4, 2, 3)), dma((4, 2, 3)), dma((4, 2, 3)),
            dma((4, 2, 3)), dma((4, 2, 3)), dma((4, 2, 3)), dma((4, 2, 3)),
            dma((4, 2, 4)), dma((4, 2, 4)), dma((4,)), dma((4,)), dma((4,)),
        ],
        compiler_params=pltpu.CompilerParams(
            collective_id=0, has_side_effects=True, vmem_limit_bytes=63 * 2**20
        ),
        cost_estimate=pl.CostEstimate(flops=flops, bytes_accessed=2**24, transcendentals=0),
    )(first, second, amp, factors)
    return spread


def home_kernel(source, kept, tiles, owned, residual, out, norms, wide):
    s = pl.program_id(0)
    for p in range(4):
        wide[p * 128:p * 128 + 128, :] = tiles[p, 0].astype(F32)
    keep = kept[s] == 1
    for a in range(VT):
        lanes = slice(a * 128, a * 128 + 128)
        ladder = wide[pl.ds(a, 4, stride=128), :]
        total = residual[0, :, lanes].astype(F32) + ladder
        out[0, :, lanes] = jnp.where(keep, total, 0.0).astype(BF)

    @pl.when(s % 4 == 0)
    def _():
        for p in range(4):
            value = owned[p, 0].astype(F32)
            mean = jnp.sum(value * value) * (1.0 / (VT * VT))
            norms[s // 4, p] = mean


def at_home(source, kept, spread, residual):
    wide_index = lax.axis_index("wide")
    owner = jnp.stack([wide_index * 2, wide_index * 2 + 1]).astype(jnp.int32)

    def kernel(source_ref, kept_ref, owner_ref, *refs):
        home_kernel(source_ref, kept_ref, *refs)

    return pl.pallas_call(
        kernel,
        out_shape=(
            jax.ShapeDtypeStruct(residual.shape, BF),
            jax.ShapeDtypeStruct((2, 4), F32),
        ),
        grid_spec=pltpu.PrefetchScalarGridSpec(
            num_scalar_prefetch=3,
            grid=(8,),
            in_specs=[
                pl.BlockSpec((4, 1, VT, VT), lambda s, src, kept, own: (0, src[s], 0, 0)),
                pl.BlockSpec((4, 1, VT, VT), lambda s, src, kept, own: (0, own[s // 4], 0, 0)),
                pl.BlockSpec((1, 4, VT * VT), lambda s, src, kept, own: (s, 0, 0)),
            ],
            out_specs=[
                pl.BlockSpec((1, 4, VT * VT), lambda s, src, kept, own: (s, 0, 0)),
                pl.BlockSpec(memory_space=pltpu.SMEM),
            ],
            scratch_shapes=[pltpu.VMEM((4 * VT, VT), F32)],
        ),
    )(source, kept, owner, spread, spread, residual)


def body(factors, t2_window, residual_in, tile_mask, owner_slot, home_slot):
    tile_ids = jnp.arange(tile_mask.shape[0], dtype=jnp.int32)
    is_filled = tile_mask == 1
    owner_match = is_filled[:, None] & (owner_slot[:, None] == jnp.arange(FILLED, dtype=jnp.int32)[None, :])
    tile_of_slot = jnp.sum(jnp.where(owner_match, tile_ids[:, None], 0), axis=0).astype(jnp.int32)
    home_ids = lax.axis_index("wide") * 8 + jnp.arange(8, dtype=jnp.int32)
    present = is_filled[:, None] & (home_slot[:, None] == home_ids[None, :])
    kept = jnp.any(present, axis=0).astype(jnp.int32)
    source = jnp.sum(jnp.where(present, owner_slot[:, None], 0), axis=0).astype(jnp.int32)
    x = lax.axis_index("narrow")
    core = lax.axis_index("wide") % 2

    def pair(offset, slot):
        return ((x + offset) % 4) * 4 + core * 2 + slot

    pairs = jnp.stack([
        pair(2, 0), pair(2, 1), pair(1, 1), pair(3, 0), pair(1, 0), pair(3, 1), pair(0, 0), pair(0, 1),
    ])
    amp = jnp.take(jnp.pad(t2_window, ((0, 0), (0, 1), (0, 1))), pairs, axis=0)
    spread = ladders(tile_of_slot // NC, tile_of_slot % NC, amp, factors)
    return at_home(source, kept, spread, residual_in)


def solution(mesh):
    in_specs = (P(None, ("wide", "narrow"), None), P(), P("wide", "narrow", None), P(), P(), P())
    out_specs = (P("wide", "narrow", None), P("wide", "narrow"))
    return jax.shard_map(body, mesh=mesh, in_specs=in_specs, out_specs=out_specs, check_vma=False)
```

time: 744 us -> 178 us (0.24)
  waiting for transfers between devices: 416 us -> 0 us
  Pallas kernels: 0 us -> 171 us
  local copies, waits for them, and re-layouts: 121 us -> 1.41 us
  matrix products: 95.4 us -> 0 us
  loops' own time: 29.6 us -> 0 us
  blocking collectives: 29.3 us -> 0 us
  other arithmetic: 22 us -> 4.71 us
  between operations: 15.1 us -> 0.73 us
  starting transfers between devices: 9.84 us -> 0 us
    all_to_all x1 -> x0, waiting for transfers between devices: 336 us -> none  [body(): lax.all_to_all(outgoing, 'wide', split_axis=0, concat_axis=0, tiled=True)]
    pallas_call x0 -> x2, Pallas kernels: none -> 171 us  [the longest x1 163 us: ladders(): pl.pallas_call(ladder_kernel, out_shape=(jax.ShapeDtypeStruct((4, FILLED,...]
    dot_general x5 -> x0, matrix products: 95.4 us -> none  [the longest x2 41.2 us: tile_contract(): lax.dot_general(first_side, second_side, (((0,), (0,)), ((), ())), prefer...]
    all_gather x1 -> x0, waiting for transfers between devices: 79.8 us -> none  [body(): gathered_rows = lax.all_gather(ladder, 'wide', axis=0, tiled=True)]
    dot_general x6 -> x0, local copies, waits for them, and re-layouts: 40.2 us -> none  [the longest x4 39.6 us: tile_contract(): lax.dot_general(first_side, second_side, (((0,), (0,)), ((), ())), prefer...]
    dynamic_update_slice x2 -> x0, local copies, waits for them, and re-layouts: 37 us -> none  [body(): lax.map(one_tile, jnp.arange(received.shape[1], dtype=jnp.int32))]
    another operation x1 -> x0, loops' own time: 29.6 us -> none  [body(): lax.map(one_tile, jnp.arange(received.shape[1], dtype=jnp.int32))]
    unnamed x1 -> x0, blocking collectives: 29.3 us -> none
  transfers between devices with their start and end apart: 2 -> 0, of which waited for: 2 -> 0; matrix products, arithmetic and copies ran while one was open for 0% -> 0% of each run, Pallas kernels for 0% -> 0%
where the time goes in v1:
time: 178 us
  Pallas kernels  171 us (96%)
  other arithmetic  4.71 us (3%)
    pallas_call x1, Pallas kernels, ladders(): pl.pallas_call(ladder_kernel, out_shape=(jax.ShapeDtypeStruct((4, FILLED,...  163 us
    pallas_call x1, Pallas kernels, at_home(): pl.pallas_call(kernel, out_shape=(jax.ShapeDtypeStruct(residual.shape, BF...  7.23 us

profile of v1, /device:TPU:1, one launch (start us, length us, event | category | flops | bytes accessed | tf_op | source)
XLA Modules:
  0.0 177.6 jit_solution(4642784367953444574)
XLA Ops:
  0.6 0.0 copy-start
  0.7 0.1 stack.65
  0.8 0.1 stack.74
  0.9 0.5 copy-done
  1.5 0.6 gather_fusion
  2.1 0.7 pad_select_fusion.amp
  2.8 0.7 broadcast_compare_fusion
  3.5 0.8 select_reduce_fusion
  4.3 0.5 and_select_fusion
  4.8 0.0 copy-start.2
  4.8 0.0 copy-start.1
  4.9 163.5 %shard_map.77 = (bf16[4,64,128,128]{3,2,1,0:T(8,128)(2,1)}, bf16[15,56,1920]{2,1,0:T(8,128)(2,1)}) custom-call(s32[64]{0:T(128)} %get-tuple-element.5.first, s32[64]{0:T(128)} %get-tuple-element.4.second, bf16[8,16,16]{2,1,0:T(8,128)(2,1)} %pad_select_fusion.amp, bf16[15,56,1920]{2,1,0:T(8,128)(2,1)} %own_rows.1), custom_call_target="tpu_custom_call" | custom-call | flops 30064771072 | bytes 16777216 | tf_op jit(solution)/shard_map/pallas_call | solution.py:394
  168.3 0.6 pad_add_fusion.owner_ref
  168.9 0.0 copy-done.2
  168.9 0.2 fusion.1
  169.1 0.5 convert_element_type.5.kept_ref
  169.7 0.0 copy-done.1
  169.7 0.7 select_reduce_fusion.1.source_ref
  170.3 7.2 %shard_map.78 = (bf16[8,4,16384]{2,1,0:T(4,128)(2,1)}, f32[2,4]{1,0:T(2,128)}) custom-call(s32[8]{0:T(128)} %select_reduce_fusion.1.source_ref, s32[8]{0:T(128)} %convert_element_type.5.kept_ref, s32[2]{0:T(128)} %pad_add_fusion.owner_ref, bf16[4,64,128,128]{3,2,1,0:T(8,128)(2,1)} %get-tuple-element.3.refs_0_.refs_1_, ...), custom_call_target="tpu_custom_call" | custom-call | tf_op jit(solution)/shard_map/pallas_call | solution.py:454
  (5 shorter events, 0.0 us)
Async XLA Ops:
  0.6 0.8 copy-start
  4.8 164.1 %copy-start.2 = (s32[225]{0:T(256)S(1)}, s32[225]{0:T(256)}, u32[]{:S(2)}) copy-start(s32[225]{0:T(256)} %param.11) | copy-start | bytes 2704
  4.8 164.8 %copy-start.1 = (s32[225]{0:T(256)S(1)}, s32[225]{0:T(256)}, u32[]{:S(2)}) copy-start(s32[225]{0:T(256)} %param.10) | copy-start | bytes 2704

commit v2 on v1

v2 whole, which is shorter than its diff:
```python
import functools

import jax
import jax.numpy as jnp
from jax import lax
from jax.experimental import pallas as pl
from jax.experimental.pallas import tpu as pltpu
from jax.sharding import PartitionSpec as P

BF = jnp.bfloat16
F32 = jnp.float32
MESH = pl.DeviceIdType.MESH
VT = 128
W = 15
NC = 15
ROWS = 56
KC = 1792
FILLED = 64
START2, START0, START1 = 0, 2, 4


def place():
    w = lax.axis_index("wide")
    return lax.axis_index("narrow"), (w // 2) % 4, w // 8, w % 2


def at(x, y, z, c):
    return {"wide": z * 8 + y * 2 + c, "narrow": x}


def ladder_kernel(
    first, second, choice, amp, own_rows,
    spread, norms, other_rows,
    weights, f2, f1t, y_buf, out, raw, rx, ry, rz, r2, r3, done_0, done_1, done_2, done_3, squares,
    ex_s, ex_r, ld_s, x_s, x_r, y_s, y_r, z_s, z_r, s2_s, s2_r, s3_s, s3_r,
    ag_s, ag_r, aa_s, aa_r, co_s, co_r, st_s, nz_s, nz_r, ny_s, ny_r, nc_s, nc_r, nl_s,
):
    x, y, z, c = place()
    done = (done_0, done_1, done_2, done_3)
    ring = {
        "x": (x, [at((x + k) % 4, y, z, c) for k in range(4)]),
        "y": (y, [at(x, (y + k) % 4, z, c) for k in range(4)]),
        "z": (z, [at(x, y, (z + k) % 4, c) for k in range(4)]),
    }
    partner = at(x, y, z, 1 - c)

    barrier = pltpu.get_barrier_semaphore()
    greeted = [partner] + [ring[a][1][k] for a in "xyz" for k in (1, 2, 3)]
    for device in greeted:
        pl.semaphore_signal(barrier, inc=1, device_id=device, device_id_type=MESH)
    pl.semaphore_wait(barrier, len(greeted))

    def remote(src, dst, s_sem, r_sem, device):
        return pltpu.make_async_remote_copy(
            src_ref=src, dst_ref=dst, send_sem=s_sem, recv_sem=r_sem, device_id=device, device_id_type=MESH
        )

    def exchange(i):
        return remote(own_rows.at[i], other_rows.at[i], ex_s.at[i], ex_r.at[i], partner)

    def start_exchange(i, _):
        exchange(i).start()
        return 0

    lax.fori_loop(0, NC, start_exchange, 0)

    row = lax.broadcasted_iota(jnp.int32, (256, 16), 0)
    col = lax.broadcasted_iota(jnp.int32, (256, 16), 1)
    widen = (row // 16 == col).astype(F32).astype(BF)
    row2 = lax.broadcasted_iota(jnp.int32, (256, 256), 0)
    col2 = lax.broadcasted_iota(jnp.int32, (256, 256), 1)
    same = row2 % 16 == col2 % 16
    for i in range(8):
        tall = jnp.dot(widen, amp[i], preferred_element_type=F32).astype(BF)
        full = lax.dot_general(tall, widen, (((1,), (1,)), ((), ())), preferred_element_type=F32)
        weights[i // 2, (i % 2) * 256:(i % 2) * 256 + 256, :] = jnp.where(same, full, 0.0).astype(BF)

    def load(which, i):
        src = (own_rows, other_rows)[which]
        return pltpu.make_async_copy(src.at[i], raw.at[which, i % 2], ld_s.at[which, i % 2])

    def start_load(i):
        load(0, i).start()
        exchange(i).wait_recv()
        load(1, i).start()

    start_load(0)
    f2[52, :, 128:256] = jnp.zeros((256, 128), BF)

    def assemble(i, _):
        @pl.when(i + 1 < NC)
        def _():
            start_load(i + 1)

        load(0, i).wait()
        load(1, i).wait()
        slot = i % 2
        for blk in range(7):
            parts = []
            for d in range(W):
                lanes = slice(d * 128, d * 128 + 128)
                if blk < 6:
                    r0 = (blk % 3) * 16
                    parts.append(raw[blk // 3, slot, r0:r0 + 16, lanes])
                else:
                    parts.append(
                        jnp.concatenate([raw[0, slot, 48:56, lanes], raw[1, slot, 48:56, lanes]], axis=0)
                    )
            parts.append(jnp.zeros((16, 128), BF))
            block = jnp.concatenate(parts, axis=0)
            f1t[i, :, blk * 256:blk * 256 + 256] = block.T
            if blk < 6:
                f2[i * 3 + blk // 2, :, (blk % 2) * 128:(blk % 2) * 128 + 128] = block
            else:
                f2[45 + i // 2, :, pl.ds(pl.multiple_of((i % 2) * 128, 128), 128)] = block
        return 0

    lax.fori_loop(0, NC, assemble, 0)

    def put(axis, view, recv, s_sem, r_sem, way, kind):
        step = 2 if kind == 0 else (1 if way == 0 else 3)
        half = {0: way, 1: 1 - way, 2: way}[kind]
        return remote(view(step, half), recv(way, kind), s_sem(way, kind), r_sem(way, kind), ring[axis][1][3 if way else 1])

    def add_tiles(dst, terms, n, own=None):
        own = dst if own is None else own

        def one(i, _):
            total = own.at[i][...].astype(F32)
            for term in terms:
                total = total + term.at[i][...].astype(F32)
            dst.at[i][...] = total.astype(BF)
            return 0

        lax.fori_loop(0, n, one, 0)

    def view1(axis, s):
        coord, base = ring[axis][0], 32 if axis == "y" else 48
        return lambda k, h: out.at[s, :, pl.ds(base + ((coord + k) % 4) * 4 + 2 * h, 2)]

    def put1(axis, s, way, kind):
        buf, ss, rs = (ry, y_s, y_r) if axis == "y" else (rz, z_s, z_r)
        return put(
            axis, view1(axis, s), lambda w, k: buf.at[w, k, s], lambda w, k: ss.at[s, w, k],
            lambda w, k: rs.at[s, w, k], way, kind,
        )

    def later1(axis, s):
        buf = ry if axis == "y" else rz
        for way in (0, 1):
            put1(axis, s, way, 0).wait_recv()
            dst = view1(axis, s)(1 if way == 0 else 3, way)
            for slot in range(2):
                add_tiles(dst.at[slot], [buf.at[way, 0, s, slot]], 2)
            put1(axis, s, way, 2).start()

    X_AT = {(0, 0): (0, 0), (1, 0): (0, 1), (0, 1): (1, 0), (1, 1): (1, 1), (0, 2): (2, 0), (1, 2): (2, 1)}

    def put_x(b, way, kind):
        s, slot = X_AT[(way, kind)]
        return remote(
            out.at[s, slot, b * 16:b * 16 + 16], rx.at[b, way, kind], x_s.at[b, way, kind], x_r.at[b, way, kind],
            ring["x"][1][3 if way else 1],
        )

    def compute(s, b):
        def group(i, _):
            for u in range(8):
                t = b * 16 + i * 8 + u
                o = jnp.dot(f1t[first[t]], y_buf[second[t]], preferred_element_type=F32).astype(BF)
                out[s, 0, t] = o[:, :128]
                out[s, 1, t] = o[:, 128:]
            return 0

        lax.fori_loop(0, 2, group, 0)

    def amplitudes(s):
        def put_block(o, i, blk, half):
            rows = slice(blk * 256, blk * 256 + 256)
            for slot in range(2):
                y_buf[i, rows, slot * 128:slot * 128 + 128] = o[slot * 256:slot * 256 + 256, half * 128:half * 128 + 128]

        def cluster(i, _):
            for j in range(3):
                o = jnp.dot(weights[s], f2[i * 3 + j], preferred_element_type=F32).astype(BF)
                for half in range(2):
                    put_block(o, i, 2 * j + half, half)
            return 0

        lax.fori_loop(0, NC, cluster, 0)

        def tail(i, _):
            o = jnp.dot(weights[s], f2[45 + i], preferred_element_type=F32).astype(BF)
            for half in range(2):
                put_block(o, 2 * i + half, 6, half)
            return 0

        lax.fori_loop(0, 7, tail, 0)
        o = jnp.dot(weights[s], f2[52], preferred_element_type=F32).astype(BF)
        put_block(o, 14, 6, 0)

    MAJOR = ("y", "z", "y", "z")
    MINOR = ("z", "y", "z", "y")

    def corner(b):
        return 16 * b, ring[MAJOR[b]][0], ring[MINOR[b]][0]

    def put2(b, s, way, kind):
        base, hi, lo = corner(b)
        return put(
            MINOR[b], lambda k, h: out.at[s, h, base + hi * 4 + (lo + k) % 4], lambda w, k: r2.at[b, w, k, s],
            lambda w, k: s2_s.at[b, s, w, k], lambda w, k: s2_r.at[b, s, w, k], way, kind,
        )

    def send1(b, s):
        for kind in (0, 1):
            for way in (0, 1):
                put1(MAJOR[b], s, way, kind).start()

    def sum1(b, s):
        base, hi, lo = corner(b)
        buf = ry if b == 2 else rz
        for way in (0, 1):
            for kind in (1, 2):
                put1(MAJOR[b], s, way, kind).wait_recv()
        for slot in range(2):
            for half in range(2):
                own = out.at[s, slot, pl.ds(base + hi * 4 + 2 * half, 2)]
                add_tiles(own, [buf.at[half, 2, s, slot], buf.at[1 - half, 1, s, slot]], 2)
        for kind in (0, 1):
            for way in (0, 1):
                put2(b, s, way, kind).start()

    def later2(b, s):
        base, hi, lo = corner(b)
        for way in (0, 1):
            put2(b, s, way, 0).wait_recv()
            dst = out.at[s, way, base + hi * 4 + (lo + (3 if way else 1)) % 4]
            dst[...] = (dst[...].astype(F32) + r2[b, way, 0, s].astype(F32)).astype(BF)
            put2(b, s, way, 2).start()

    def sum2(b, s):
        base, hi, lo = corner(b)
        for way in (0, 1):
            for kind in (1, 2):
                put2(b, s, way, kind).wait_recv()
        for h in range(2):
            dst = out.at[s, h, base + hi * 4 + lo]
            total = dst[...].astype(F32) + r2[b, h, 2, s].astype(F32) + r2[b, 1 - h, 1, s].astype(F32)
            dst[...] = total.astype(BF)

    ACTS = (send1, lambda b, s: later1(MAJOR[b], s), sum1, later2, sum2)

    def step(s, _):
        amplitudes(s)
        for b in (0, 1):
            compute(s, b)

            @pl.when(s == 0)
            def _():
                for way in (0, 1):
                    put_x(b, way, 0).start()

            @pl.when(s == 1)
            def _():
                for way in (0, 1):
                    put_x(b, way, 1).start()

            @pl.when(s == 2)
            def _():
                for way in (0, 1):
                    put_x(b, way, 0).wait_recv()
                    add_tiles(out.at[2, way, b * 16:b * 16 + 16], [rx.at[b, way, 0]], 16)
                    put_x(b, way, 2).start()

        for b in (2, 3):
            compute(s, b)
            ACTS[0](b, s)
            for n in (1, 2, 3):
                @pl.when(s >= n)
                def _():
                    ACTS[n](b, s - n)
        return 0

    lax.fori_loop(0, 4, step, 0)

    def put2x(b, way, kind):
        base, hi, lo = corner(b)
        return put(
            MAJOR[b], lambda k, h: out.at[3, h, pl.ds(base + ((hi + k) % 4) * 4, 4)], lambda w, k: r2.at[b, w, k],
            lambda w, k: s2_s.at[b, 0, w, k], lambda w, k: s2_r.at[b, 0, w, k], way, kind,
        )

    PLANES = {1: ((2, 0), (1, 0)), 2: ((0, 0), (0, 1)), 3: ((1, 1), (2, 1))}

    def put3(b, k, h):
        base, hi, lo = corner(b)
        if b < 2:
            src, axis = out.at[3, h, base + hi * 4 + (lo + k) % 4], MINOR[b]
        else:
            s, slot = PLANES[k][h]
            src, axis = out.at[s, slot, base + hi * 4 + lo], "x"
        return remote(src, r3.at[b, k - 1, h], s3_s.at[b, k - 1, h], s3_r.at[b, k - 1, h], ring[axis][1][k])

    def share(b, k):
        base, hi, lo = corner(b)
        return remote(done[b].at[lo], done[b].at[lo], ag_s.at[b, k - 1], ag_r.at[b, k - 1], ring[MINOR[b]][1][k])

    def packed(b, k):
        return rx.at[b // 2, b % 2, 0, 2 * k:2 * k + 2]

    def deliver(b, k):
        base, hi, lo = corner(b)
        cell = spread.at[c, 4 * b + hi]
        if k == 0:
            return pltpu.make_async_copy(packed(b, 0), cell, st_s.at[b])
        return remote(packed(b, k), cell, aa_s.at[b, k - 1], aa_r.at[b, k - 1], ring[MAJOR[b]][1][k])

    def core_copy(b):
        rows = spread.at[c, 4 * b:4 * b + 4]
        return remote(rows, rows, co_s.at[b], co_r.at[b], partner)

    def batch(b):
        base, hi, lo = corner(b)
        if b < 2:
            for way in (0, 1):
                for kind in (1, 2):
                    put_x(b, way, kind).wait_recv()
            for half in range(2):
                add_tiles(out.at[3, half, base:base + 16], [rx.at[b, half, 2], rx.at[b, 1 - half, 1]], 16)
            for kind in (0, 1):
                for way in (0, 1):
                    put2x(b, way, kind).start()
            yield
            for way in (0, 1):
                put2x(b, way, 0).wait_recv()
                near = pl.ds(base + ((hi + (3 if way else 1)) % 4) * 4, 4)
                add_tiles(out.at[3, way, near], [r2.at[b, way, 0]], 4)
                put2x(b, way, 2).start()
            yield
            for way in (0, 1):
                for kind in (1, 2):
                    put2x(b, way, kind).wait_recv()
            for half in range(2):
                add_tiles(out.at[3, half, pl.ds(base + hi * 4, 4)], [r2.at[b, half, 2], r2.at[b, 1 - half, 1]], 4)
        else:
            for turn in range(4):
                for n in (1, 2, 3, 4):
                    s = turn + 4 - n
                    if s < 4:
                        ACTS[n](b, s)
                if turn < 3:
                    yield
        for k in (2, 1, 3):
            for h in range(2):
                put3(b, k, h).start()
        yield
        for k in (1, 2, 3):
            for h in range(2):
                put3(b, k, h).wait_recv()
        for h in range(2):
            total = out[3, h, base + hi * 4 + lo].astype(F32)
            for k in range(3):
                total = total + r3[b, k, h].astype(F32)
            tile = total.astype(BF)
            done[b][lo, h] = tile
            value = tile.astype(F32)
            mean = jnp.sum(value * value, keepdims=True) * (1.0 / (VT * VT))
            squares[c, z, y, 2 * b + h:2 * b + h + 1, :] = jnp.broadcast_to(mean, (1, 128))
        for k in (2, 1, 3):
            share(b, k).start()
        yield
        for k in (1, 2, 3):
            share(b, k).wait_recv()
        for k in (2, 1, 3, 0):
            for h in range(2):
                rx[b // 2, b % 2, 0, 2 * k + h] = done[b][choice[4 * b + k], h]
            deliver(b, k).start()
        yield
        deliver(b, 0).wait()
        for k in (1, 2, 3):
            deliver(b, k).wait_recv()
        core_copy(b).start()

    def norms_z(k):
        part = squares.at[c, z, y]
        return remote(part, part, nz_s.at[k - 1], nz_r.at[k - 1], ring["z"][1][k])

    def norms_y(k):
        part = squares.at[c, :, y]
        return remote(part, part, ny_s.at[k - 1], ny_r.at[k - 1], ring["y"][1][k])

    def norms_core():
        return remote(squares.at[c], norms.at[c], nc_s, nc_r, partner)

    def all_norms():
        for k in (1, 2, 3):
            norms_z(k).start()
        yield
        for k in (1, 2, 3):
            norms_z(k).wait_recv()
        for k in (1, 2, 3):
            norms_y(k).start()
        yield
        for k in (1, 2, 3):
            norms_y(k).wait_recv()
        norms_core().start()
        keep = pltpu.make_async_copy(squares.at[c], norms.at[c], nl_s)
        keep.start()
        yield
        keep.wait()
        norms_core().wait_recv()

    order = [(START2, batch(2)), (START2, batch(3)), (START0, batch(0)), (START1, batch(1))]
    waiting = list(order)
    running = []
    turn = 0
    ready = False
    while waiting or running:
        running += [chain for when, chain in waiting if when <= turn]
        waiting = [(when, chain) for when, chain in waiting if when > turn]
        for chain in list(running):
            try:
                next(chain)
            except StopIteration:
                running.remove(chain)
        turn += 1
        if not ready and turn == START1 + 4:
            running.append(all_norms())
            ready = True
    for b in range(4):
        core_copy(b).wait_recv()

    def wait_exchange(i, _):
        exchange(i).wait_send()
        return 0

    lax.fori_loop(0, NC, wait_exchange, 0)

    def wait_steps(s, _):
        for way in (0, 1):
            for kind in range(3):
                for axis in "yz":
                    put1(axis, s, way, kind).wait_send()
                for b in (2, 3):
                    put2(b, s, way, kind).wait_send()
        return 0

    lax.fori_loop(0, 4, wait_steps, 0)
    for b in range(4):
        for way in (0, 1):
            for kind in range(3):
                if b < 2:
                    put_x(b, way, kind).wait_send()
                    put2x(b, way, kind).wait_send()
        for k in (1, 2, 3):
            for h in range(2):
                put3(b, k, h).wait_send()
            share(b, k).wait_send()
            deliver(b, k).wait_send()
        core_copy(b).wait_send()
    for k in (1, 2, 3):
        norms_z(k).wait_send()
        norms_y(k).wait_send()
    norms_core().wait_send()


def ladders(first, second, choice, amp, factors):
    dma = pltpu.SemaphoreType.DMA
    any_space = pl.BlockSpec(memory_space=pl.ANY)
    smem = pl.BlockSpec(memory_space=pltpu.SMEM)
    vmem = pl.BlockSpec(memory_space=pltpu.VMEM)
    flops = 2 * FILLED * 8 * VT * VT * KC
    spread, norms, _ = pl.pallas_call(
        ladder_kernel,
        out_shape=(
            jax.ShapeDtypeStruct((2, 16, 2, VT, VT), BF),
            jax.ShapeDtypeStruct((2, 4, 4, 8, 128), F32),
            jax.ShapeDtypeStruct(factors.shape, BF),
        ),
        in_specs=[smem, smem, smem, vmem, any_space],
        out_specs=(any_space, any_space, any_space),
        scratch_shapes=[
            pltpu.VMEM((4, 512, 256), BF),
            pltpu.VMEM((53, 256, 256), BF),
            pltpu.VMEM((NC, VT, KC), BF),
            pltpu.VMEM((NC, KC, 256), BF),
            pltpu.VMEM((4, 2, FILLED, VT, VT), BF),
            pltpu.VMEM((2, 2, ROWS, W * VT), BF),
            pltpu.VMEM((2, 2, 3, 16, VT, VT), BF),
            pltpu.VMEM((2, 3, 4, 2, 2, VT, VT), BF),
            pltpu.VMEM((2, 3, 4, 2, 2, VT, VT), BF),
            pltpu.VMEM((4, 2, 3, 4, VT, VT), BF),
            pltpu.VMEM((4, 3, 2, VT, VT), BF),
            pltpu.VMEM((4, 2, VT, VT), BF),
            pltpu.VMEM((4, 2, VT, VT), BF),
            pltpu.VMEM((4, 2, VT, VT), BF),
            pltpu.VMEM((4, 2, VT, VT), BF),
            pltpu.VMEM((2, 4, 4, 8, 128), F32),
            dma((NC,)), dma((NC,)), dma((2, 2)),
            dma((2, 2, 3)), dma((2, 2, 3)),
            dma((4, 2, 3)), dma((4, 2, 3)), dma((4, 2, 3)), dma((4, 2, 3)),
            dma((4, 4, 2, 3)), dma((4, 4, 2, 3)), dma((4, 3, 2)), dma((4, 3, 2)),
            dma((4, 3)), dma((4, 3)), dma((4, 3)), dma((4, 3)),
            dma((4,)), dma((4,)), dma((4,)),
            dma((3,)), dma((3,)), dma((3,)), dma((3,)), dma, dma, dma,
        ],
        compiler_params=pltpu.CompilerParams(
            collective_id=0, has_side_effects=True, vmem_limit_bytes=63 * 2**20
        ),
        cost_estimate=pl.CostEstimate(flops=flops, bytes_accessed=2**24, transcendentals=0),
    )(first, second, choice, amp, factors)
    return spread, norms


def home_kernel(source, kept, norm_row, tiles, norms, residual, out, norms_out, wide):
    s = pl.program_id(0)
    for p in range(4):
        wide[p * 128:p * 128 + 128, :] = tiles[p // 2, 0, p % 2].astype(F32)
    keep = kept[s] == 1
    for a in range(VT):
        lanes = slice(a * 128, a * 128 + 128)
        ladder = wide[pl.ds(a, 4, stride=128), :]
        total = residual[0, :, lanes].astype(F32) + ladder
        out[0, :, lanes] = jnp.where(keep, total, 0.0).astype(BF)

    @pl.when(s == 0)
    def _():
        for i in range(2):
            for p in range(4):
                row = norms[pl.ds((p // 2) * 128 + norm_row[i] + p % 2, 1), :]
                norms_out[i, p] = jnp.max(row)


def at_home(source, kept, norm_row, spread, norms, residual):
    return pl.pallas_call(
        home_kernel,
        out_shape=(
            jax.ShapeDtypeStruct(residual.shape, BF),
            jax.ShapeDtypeStruct((2, 4), F32),
        ),
        grid_spec=pltpu.PrefetchScalarGridSpec(
            num_scalar_prefetch=3,
            grid=(8,),
            in_specs=[
                pl.BlockSpec((2, 1, 2, VT, VT), lambda s, src, kept, row: (0, src[s], 0, 0, 0)),
                pl.BlockSpec((256, 128), lambda s, src, kept, row: (0, 0)),
                pl.BlockSpec((1, 4, VT * VT), lambda s, src, kept, row: (s, 0, 0)),
            ],
            out_specs=[
                pl.BlockSpec((1, 4, VT * VT), lambda s, src, kept, row: (s, 0, 0)),
                pl.BlockSpec(memory_space=pltpu.SMEM),
            ],
            scratch_shapes=[pltpu.VMEM((4 * VT, VT), F32)],
        ),
    )(source, kept, norm_row, spread, norms.reshape(256, 128), residual)


def body(factors, t2_window, residual_in, tile_mask, owner_slot, home_slot):
    x = lax.axis_index("narrow")
    wide_index = lax.axis_index("wide")
    core, own_y, own_z = wide_index % 2, (wide_index // 2) % 4, wide_index // 8
    filled = tile_mask == 1
    ids = jnp.arange(tile_mask.shape[0], dtype=jnp.int32)
    before = filled[None, :] & (home_slot[None, :] < home_slot[:, None])
    place_of = jnp.sum(before.astype(jnp.int32), axis=1)
    index_of = (place_of % 16) * 4 + place_of // 16
    match = filled[:, None] & (index_of[:, None] == jnp.arange(FILLED, dtype=jnp.int32)[None, :])
    tile_at = jnp.sum(jnp.where(match, ids[:, None], 0), axis=0).astype(jnp.int32)
    chip_at = (jnp.sum(jnp.where(match, home_slot[:, None], 0), axis=0) // 16).reshape(4, 4, 4)
    by_y = jnp.arange(4, dtype=jnp.int32) % 2 == 0
    group = jnp.where(by_y, own_y, own_z)
    cell_chips = jnp.sum(
        jnp.where(jnp.arange(4, dtype=jnp.int32)[None, :, None] == group[:, None, None], chip_at, 0), axis=1
    )
    far = (group[:, None] + jnp.arange(4, dtype=jnp.int32)[None, :]) % 4
    target = jnp.where(by_y[:, None], own_z * 4 + far, far * 4 + own_y)
    choice = jnp.sum(
        jnp.where(cell_chips[:, None, :] == target[:, :, None], jnp.arange(4, dtype=jnp.int32)[None, None, :], 0),
        axis=2,
    ).astype(jnp.int32).reshape(16)
    home_ids = wide_index * 8 + jnp.arange(8, dtype=jnp.int32)
    present = filled[:, None] & (home_slot[:, None] == home_ids[None, :])
    kept = jnp.any(present, axis=0).astype(jnp.int32)
    source = jnp.sum(jnp.where(present, index_of[:, None] // 4, 0), axis=0).astype(jnp.int32)
    owner_ids = wide_index * 2 + jnp.arange(2, dtype=jnp.int32)
    owned = filled[:, None] & (owner_slot[:, None] == owner_ids[None, :])
    batch, grp, turn = index_of // 16, (index_of // 4) % 4, index_of % 4
    row_of = jnp.where(batch % 2 == 0, turn * 4 + grp, grp * 4 + turn) * 8 + 2 * batch
    norm_row = jnp.sum(jnp.where(owned, row_of[:, None], 0), axis=0).astype(jnp.int32)

    def pair(offset, slot):
        return ((x + offset) % 4) * 4 + core * 2 + slot

    pairs = jnp.stack([
        pair(2, 0), pair(2, 1), pair(1, 1), pair(3, 0), pair(1, 0), pair(3, 1), pair(0, 0), pair(0, 1),
    ])
    amp = jnp.take(jnp.pad(t2_window, ((0, 0), (0, 1), (0, 1))), pairs, axis=0)
    spread, norms = ladders(tile_at // NC, tile_at % NC, choice, amp, factors)
    return at_home(source, kept, norm_row, spread, norms, residual_in)


def solution(mesh):
    in_specs = (P(None, ("wide", "narrow"), None), P(), P("wide", "narrow", None), P(), P(), P())
    out_specs = (P("wide", "narrow", None), P("wide", "narrow"))
    return jax.shard_map(body, mesh=mesh, in_specs=in_specs, out_specs=out_specs, check_vma=False)
```

time: 178 us -> 182 us (1.022)
  other arithmetic: 4.71 us -> 8.41 us
    reduce_sum x2 -> x6, other arithmetic: 1.46 us -> 4.85 us  [the longest x1 1.4 us: body(): jnp.sum(jnp.where(owned, row_of[:, None], 0), axis=0).astype(jnp.int32)]
where the time goes in v2:
time: 182 us; the launch traced here: 181 us
  Pallas kernels  171 us (94%)
  other arithmetic  8.41 us (5%)
    pallas_call x1, Pallas kernels, ladders(): pl.pallas_call(ladder_kernel, out_shape=(jax.ShapeDtypeStruct((2, 16, 2,...  164 us
    pallas_call x1, Pallas kernels, at_home(): pl.pallas_call(home_kernel, out_shape=(jax.ShapeDtypeStruct(residual.shap...  7 us

profile of v2, /device:TPU:1, one launch (start us, length us, event | category | flops | bytes accessed | tf_op | source)
XLA Modules:
  0.0 181.4 jit_solution(5814180857237860513)
XLA Ops:
  0.6 0.0 copy-start
  0.8 0.7 broadcast_compare_fusion
  1.5 0.9 fusion.5
  2.3 0.5 convert_element_type.9.kept
  2.9 0.1 iota_compare_fusion.1
  2.9 0.1 stack.53
  3.0 0.1 stack.62
  3.2 0.1 add_select_fusion.2
  3.2 0.9 convert_reduce_fusion
  4.2 1.4 fusion.6.norm_row
  5.6 1.4 select_reduce_fusion.3.source
  7.0 0.8 select_reduce_fusion
  7.8 0.5 and_select_fusion.2
  8.4 0.1 reduce_sum.70
  8.4 0.1 fusion.3
  8.5 0.2 select_reduce_fusion.2
  8.8 0.7 reshape.591.choice
  9.4 0.0 copy-done
  9.4 0.7 gather_fusion
  10.1 0.7 pad_select_fusion.amp
  10.8 163.6 %shard_map.77 = (bf16[2,16,2,128,128]{4,3,2,1,0:T(8,128)(2,1)}, f32[2,4,4,8,128]{4,3,2,1,0:T(8,128)}, bf16[15,56,1920]{2,1,0:T(8,128)(2,1)}) custom-call(s32[64]{0:T(128)} %get-tuple-element.12.first, s32[64]{0:T(128)} %get-tuple-element.11.second, s32[16]{0:T(128)} %reshape.591.choice, bf16[8,16,16]{2,1,0:T(8,128)(2,1)} %pad_select_fusion.amp, ...), custom_call_target="tpu_custom_call" | custom-call | flops 30064771072 | bytes 16777216 | tf_op jit(solution)/shard_map/pallas_call | solution.py:474
  174.4 7.0 %shard_map.78 = (bf16[8,4,16384]{2,1,0:T(4,128)(2,1)}, f32[2,4]{1,0:T(2,128)}) custom-call(s32[8]{0:T(128)} %select_reduce_fusion.3.source, s32[8]{0:T(128)} %convert_element_type.9.kept, s32[2]{0:T(128)} %fusion.6.norm_row, bf16[2,16,2,128,128]{4,3,2,1,0:T(8,128)(2,1)} %get-tuple-element.4.tiles, f32[256,128]{1,0:T(8,128)} %bitcast.19, ...), custom_call_target="tpu_custom_call" | custom-call | tf_op jit(solution)/shard_map/pallas_call | solution.py:536
  (9 shorter events, 0.1 us)
Async XLA Ops:
  0.6 8.8 %copy-start = (bf16[16,15,15]{2,0,1:T(8,128)(2,1)S(1)}, bf16[16,15,15]{2,0,1:T(8,128)(2,1)}, u32[]{:S(2)}) copy-start(bf16[16,15,15]{2,0,1:T(8,128)(2,1)} %param.7) | copy-start | bytes 21604

commit v3 on v0

v3 whole, which is shorter than its diff:
```python
import functools

import jax
import jax.numpy as jnp
from jax import lax
from jax.experimental import pallas as pl
from jax.experimental.pallas import tpu as pltpu
from jax.sharding import PartitionSpec as P

BF = jnp.bfloat16
F32 = jnp.float32
I32 = jnp.int32
MESH = pl.DeviceIdType.MESH
VT = 128
W = 15
NC = 15
NT = 225
ROWS = 56
KC = 1792
FILLED = 64
MAJOR = ("y", "z", "y", "z")
MINOR = ("z", "y", "z", "y")
UNITS = [(b, p) for p in (0, 1) for b in range(4)]
X_FIRST = {(0, 0), (1, 0), (0, 1), (1, 1)}


X_WHEN = {
    (0, 0): (0, 4, 11, 12, 13),
    (1, 0): (1, 5, 12, 13, 14),
    (0, 1): (8, 12, 17, 18, 19),
    (1, 1): (9, 13, 17, 18, 19),
}
M_GAP = 2
REST_GAP = 1


def place():
    w = lax.axis_index("wide")
    return lax.axis_index("narrow"), (w // 2) % 4, w // 8, w % 2


def at(x, y, z, c):
    return {"wide": z * 8 + y * 2 + c, "narrow": x}


def ladder_kernel(plan, t2, own_rows, spread, norms, other_rows, *scratch):
    weights, f2, f1t, y_buf, out, raw, r1, r2, r3 = scratch[:9]
    done = dict(zip(UNITS, scratch[9:17]))
    (squares, ex_s, ex_r, ld_s, s1_s, s1_r, s2_s, s2_r, s3_s, s3_r, ag_s, ag_r, aa_s, aa_r, co_s, co_r, st_s,
     nz_s, nz_r, ny_s, ny_r, nc_s, nc_r, nl_s) = scratch[17:]
    x, y, z, c = place()
    ring = {
        "x": (x, [at((x + k) % 4, y, z, c) for k in range(4)]),
        "y": (y, [at(x, (y + k) % 4, z, c) for k in range(4)]),
        "z": (z, [at(x, y, (z + k) % 4, c) for k in range(4)]),
    }
    partner = at(x, y, z, 1 - c)

    barrier = pltpu.get_barrier_semaphore()
    greeted = [partner] + [ring[a][1][k] for a in "xyz" for k in (1, 2, 3)]
    for device in greeted:
        pl.semaphore_signal(barrier, inc=1, device_id=device, device_id_type=MESH)
    pl.semaphore_wait(barrier, len(greeted))

    def remote(src, dst, s_sem, r_sem, device):
        return pltpu.make_async_remote_copy(
            src_ref=src, dst_ref=dst, send_sem=s_sem, recv_sem=r_sem, device_id=device, device_id_type=MESH
        )

    def exchange(i):
        return remote(own_rows.at[i], other_rows.at[i], ex_s.at[i], ex_r.at[i], partner)

    def start_exchange(i, _):
        exchange(i).start()
        return 0

    lax.fori_loop(0, NC, start_exchange, 0)

    def load(which, i):
        src = (own_rows, other_rows)[which]
        return pltpu.make_async_copy(src.at[i], raw.at[which, i % 3], ld_s.at[which, i % 3])

    load(0, 0).start()
    load(0, 1).start()

    row = lax.broadcasted_iota(I32, (256, W), 0)
    col = lax.broadcasted_iota(I32, (256, W), 1)
    widen = (row // 16 == col).astype(F32).astype(BF)
    row2 = lax.broadcasted_iota(I32, (256, 256), 0)
    col2 = lax.broadcasted_iota(I32, (256, 256), 1)
    same = row2 % 16 == col2 % 16
    for s in range(4):
        for slot in range(2):
            ahead = (2, 1, 3, 0)[(s % 2) * 2 + slot]
            pair = ((x + ahead) % 4) * 4 + c * 2 + s // 2
            tall = jnp.dot(widen, t2[pair], preferred_element_type=F32).astype(BF)
            full = lax.dot_general(tall, widen, (((1,), (1,)), ((), ())), preferred_element_type=F32)
            weights[s, slot * 256:slot * 256 + 256, :] = jnp.where(same, full, 0.0).astype(BF)
    f2[52, :, 128:256] = jnp.zeros((256, 128), BF)

    def assemble(i, blocks):
        slot = i % 3
        for blk in blocks:
            parts = []
            for d in range(W):
                lanes = slice(d * 128, d * 128 + 128)
                if blk < 6:
                    r0 = (blk % 3) * 16
                    parts.append(raw[blk // 3, slot, r0:r0 + 16, lanes])
                else:
                    parts.append(
                        jnp.concatenate([raw[0, slot, 48:56, lanes], raw[1, slot, 48:56, lanes]], axis=0)
                    )
            parts.append(jnp.zeros((16, 128), BF))
            block = jnp.concatenate(parts, axis=0)
            f1t[i, :, blk * 256:blk * 256 + 256] = block.T
            if blk < 6:
                f2[i * 3 + blk // 2, :, (blk % 2) * 128:(blk % 2) * 128 + 128] = block
            else:
                f2[45 + i // 2, :, pl.ds(pl.multiple_of((i % 2) * 128, 128), 128)] = block

    def assemble_own(i, _):
        @pl.when(i + 2 < NC)
        def _():
            load(0, i + 2).start()

        load(0, i).wait()
        assemble(i, (0, 1, 2))
        return 0

    lax.fori_loop(0, NC, assemble_own, 0)

    def put_block(o, i, blk, half):
        rows = slice(blk * 256, blk * 256 + 256)
        for slot in range(2):
            y_buf[i, rows, slot * 128:slot * 128 + 128] = o[slot * 256:slot * 256 + 256, half * 128:half * 128 + 128]

    def amplitude_pairs(s, pairs):
        def cluster(n, _):
            for u in range(3):
                for j in pairs:
                    i = n * 3 + u
                    o = jnp.dot(weights[s], f2[i * 3 + j], preferred_element_type=F32).astype(BF)
                    for half in range(2):
                        put_block(o, i, 2 * j + half, half)
            return 0

        lax.fori_loop(0, NC // 3, cluster, 0)

    def amplitude_last(s):
        for i in range(8):
            o = jnp.dot(weights[s], f2[45 + i], preferred_element_type=F32).astype(BF)
            for half in range(2):
                if 2 * i + half < NC:
                    put_block(o, 2 * i + half, 6, half)

    amplitude_pairs(0, (0,))

    def start_both(i):
        load(0, i).start()
        exchange(i).wait_recv()
        load(1, i).start()

    start_both(0)
    start_both(1)

    def assemble_other(i, _):
        @pl.when(i + 2 < NC)
        def _():
            start_both(i + 2)

        load(0, i).wait()
        load(1, i).wait()
        assemble(i, (3, 4, 5, 6))
        return 0

    lax.fori_loop(0, NC, assemble_other, 0)

    def compute(s, b):
        for i in range(16):
            t = b * 16 + i
            o = jnp.dot(f1t[plan[0, t]], y_buf[plan[1, t]], preferred_element_type=F32).astype(BF)
            out[s, 0, t] = o[:, :128]
            out[s, 1, t] = o[:, 128:]

    def add_tiles(dst, terms, n):
        def one(i, _):
            total = dst.at[i][...].astype(F32)
            for term in terms:
                total = total + term.at[i][...].astype(F32)
            dst.at[i][...] = total.astype(BF)
            return 0

        lax.fori_loop(0, n, one, 0)

    def route(way, kind):
        return (2 if kind == 0 else (3 if way else 1)), (1 - way if kind == 1 else way)

    def corner(b):
        return 16 * b, ring[MAJOR[b]][0], ring[MINOR[b]][0]

    def number(unit):
        return unit[1] * 4 + unit[0]

    PLANE = {2: (0, 0), 1: (0, 1), 3: (1, 0), 0: (1, 1)}

    def x_part(unit, k, half):
        b, p = unit
        s, slot = PLANE[k]
        return out.at[2 * p + s, slot, 16 * b + 8 * half:16 * b + 8 * half + 8]

    def x_put(unit, way, kind):
        u = number(unit)
        return remote(
            x_part(unit, *route(way, kind)), r1.at[u, way, kind], s1_s.at[u, way, kind, 0],
            s1_r.at[u, way, kind, 0], ring["x"][1][3 if way else 1],
        )

    def x_begin(unit):
        x_put(unit, 0, 0).start()
        x_put(unit, 1, 0).start()
        x_put(unit, 0, 1).start()

    def x_pass(unit):
        x_put(unit, 1, 1).start()
        for way in (0, 1):
            x_put(unit, way, 0).wait_recv()
            add_tiles(x_part(unit, *route(way, 2)), [r1.at[number(unit), way, 0]], 8)
            x_put(unit, way, 2).start()

    def x_sum(unit):
        u = number(unit)
        for way in (0, 1):
            for kind in (1, 2):
                x_put(unit, way, kind).wait_recv()
        for half in range(2):
            add_tiles(x_part(unit, 0, half), [r1.at[u, half, 2], r1.at[u, 1 - half, 1]], 8)
        for kind in (0, 1):
            for way in (0, 1):
                x2_put(unit, way, kind).start()

    def x2_part(unit, k, half):
        b, p = unit
        base, hi, lo = corner(b)
        return out.at[2 * p + 1, 1, pl.ds(base + ((hi + k) % 4) * 4 + 2 * half, 2)]

    def x2_put(unit, way, kind):
        u = number(unit)
        return remote(
            x2_part(unit, *route(way, kind)), r2.at[u, way, kind], s2_s.at[u, way, kind, 0],
            s2_r.at[u, way, kind, 0], ring[MAJOR[unit[0]]][1][3 if way else 1],
        )

    def x2_pass(unit):
        for way in (0, 1):
            x2_put(unit, way, 0).wait_recv()
            add_tiles(x2_part(unit, *route(way, 2)), [r2.at[number(unit), way, 0]], 2)
            x2_put(unit, way, 2).start()

    def x2_sum(unit):
        u = number(unit)
        for way in (0, 1):
            for kind in (1, 2):
                x2_put(unit, way, kind).wait_recv()
        for half in range(2):
            add_tiles(x2_part(unit, 0, half), [r2.at[u, half, 2], r2.at[u, 1 - half, 1]], 2)
        last_send(unit)

    def m_part(unit, s, k, half):
        b, p = unit
        base, hi, lo = corner(b)
        return out.at[2 * p + s, :, pl.ds(base + ((hi + k) % 4) * 4 + 2 * half, 2)]

    def m_land(unit, s, way, kind):
        return r1.at[number(unit), way, kind, 4 * s:4 * s + 4]

    def m_put(unit, s, slot, way, kind):
        u = number(unit)
        return remote(
            m_part(unit, s, *route(way, kind)).at[slot], m_land(unit, s, way, kind).at[2 * slot:2 * slot + 2],
            s1_s.at[u, way, kind, 2 * s + slot], s1_r.at[u, way, kind, 2 * s + slot],
            ring[MAJOR[unit[0]]][1][3 if way else 1],
        )

    def m_begin(unit, s):
        for kind in (0, 1):
            for way in (0, 1):
                for slot in range(2):
                    m_put(unit, s, slot, way, kind).start()

    def m_pass(unit, s):
        for way in (0, 1):
            for slot in range(2):
                m_put(unit, s, slot, way, 0).wait_recv()
                add_tiles(
                    m_part(unit, s, *route(way, 2)).at[slot], [m_land(unit, s, way, 0).at[2 * slot:2 * slot + 2]], 2
                )
                m_put(unit, s, slot, way, 2).start()

    def m_sum(unit, s):
        for way in (0, 1):
            for kind in (1, 2):
                for slot in range(2):
                    m_put(unit, s, slot, way, kind).wait_recv()
        for half in range(2):
            for slot in range(2):
                two = slice(2 * slot, 2 * slot + 2)
                add_tiles(
                    m_part(unit, s, 0, half).at[slot],
                    [m_land(unit, s, half, 2).at[two], m_land(unit, s, 1 - half, 1).at[two]], 2,
                )
        for kind in (0, 1):
            for way in (0, 1):
                m2_put(unit, s, way, kind).start()

    def m2_part(unit, s, k, half):
        b, p = unit
        base, hi, lo = corner(b)
        return out.at[2 * p + s, half, base + hi * 4 + (lo + k) % 4]

    def m2_put(unit, s, way, kind):
        u = number(unit)
        return remote(
            m2_part(unit, s, *route(way, kind)), r2.at[u, way, kind, s], s2_s.at[u, way, kind, s],
            s2_r.at[u, way, kind, s], ring[MINOR[unit[0]]][1][3 if way else 1],
        )

    def m2_pass(unit, s):
        for way in (0, 1):
            m2_put(unit, s, way, 0).wait_recv()
            dst = m2_part(unit, s, *route(way, 2))
            dst[...] = (dst[...].astype(F32) + r2[number(unit), way, 0, s].astype(F32)).astype(BF)
            m2_put(unit, s, way, 2).start()

    def m2_sum(unit, s):
        u = number(unit)
        for way in (0, 1):
            for kind in (1, 2):
                m2_put(unit, s, way, kind).wait_recv()
        for half in range(2):
            dst = m2_part(unit, s, 0, half)
            total = dst[...].astype(F32) + r2[u, half, 2, s].astype(F32) + r2[u, 1 - half, 1, s].astype(F32)
            dst[...] = total.astype(BF)
        if s == 1:
            last_send(unit)

    def last_part(unit, k):
        b, p = unit
        base, hi, lo = corner(b)
        if unit in X_FIRST:
            return out.at[2 * p + 1, 1, base + hi * 4 + (lo + k) % 4]
        s, slot = PLANE[k]
        return out.at[2 * p + s, slot, base + hi * 4 + lo]

    def last_put(unit, k):
        u = number(unit)
        axis = MINOR[unit[0]] if unit in X_FIRST else "x"
        return remote(last_part(unit, k), r3.at[u, k - 1], s3_s.at[u, k - 1], s3_r.at[u, k - 1], ring[axis][1][k])

    def last_send(unit):
        for k in (2, 1, 3):
            last_put(unit, k).start()

    def last_sum(unit):
        b, p = unit
        u = number(unit)
        base, hi, lo = corner(b)
        for k in (1, 2, 3):
            last_put(unit, k).wait_recv()
        total = last_part(unit, 0)[...].astype(F32)
        for k in range(3):
            total = total + r3[u, k].astype(F32)
        tile = total.astype(BF)
        done[unit][lo] = tile
        for k in (2, 1, 3):
            share(unit, k).start()
        value = tile.astype(F32)
        mean = jnp.sum(value * value, keepdims=True) * (1.0 / (VT * VT))
        squares[c, z, y, 2 * b + p:2 * b + p + 1, :] = jnp.broadcast_to(mean, (1, 128))

    def share(unit, k):
        u = number(unit)
        lo = corner(unit[0])[2]
        return remote(
            done[unit].at[lo], done[unit].at[lo], ag_s.at[u, k - 1], ag_r.at[u, k - 1], ring[MINOR[unit[0]]][1][k]
        )

    def packed(unit, k):
        return r1.at[number(unit), 0, 0, k]

    def deliver(unit, k):
        b, p = unit
        u = number(unit)
        cell = spread.at[c, p, 4 * b + corner(b)[1]]
        if k == 0:
            return pltpu.make_async_copy(packed(unit, 0), cell, st_s.at[u])
        return remote(packed(unit, k), cell, aa_s.at[u, k - 1], aa_r.at[u, k - 1], ring[MAJOR[b]][1][k])

    def handout(unit):
        b, p = unit
        for k in (1, 2, 3):
            share(unit, k).wait_recv()
        for k in (2, 1, 3, 0):
            r1[number(unit), 0, 0, k] = done[unit][plan[2, 4 * b + k]]
            deliver(unit, k).start()

    def core_copy(unit):
        b, p = unit
        rows = spread.at[c, p, 4 * b:4 * b + 4]
        return remote(rows, rows, co_s.at[number(unit)], co_r.at[number(unit)], partner)

    def finish(unit):
        deliver(unit, 0).wait()
        for k in (1, 2, 3):
            deliver(unit, k).wait_recv()
        core_copy(unit).start()

    def phases(unit):
        bind = functools.partial
        if unit in X_FIRST:
            first = [bind(f, unit) for f in (x_begin, x_pass, x_sum, x2_pass, x2_sum)]
        else:
            acts = (m_begin, m_pass, m_sum, m2_pass, m2_sum)
            first = [[bind(f, unit, s) for f in acts] for s in (0, 1)]
        return first, [bind(f, unit) for f in (last_sum, handout, finish)]

    def norms_z(k):
        part = squares.at[c, z, y]
        return remote(part, part, nz_s.at[k - 1], nz_r.at[k - 1], ring["z"][1][k])

    def norms_y(k):
        part = squares.at[c, :, y]
        return remote(part, part, ny_s.at[k - 1], ny_r.at[k - 1], ring["y"][1][k])

    def norms_core():
        return remote(squares.at[c], norms.at[c], nc_s, nc_r, partner)

    def norms_keep():
        return pltpu.make_async_copy(squares.at[c], norms.at[c], nl_s)

    def norms_begin():
        for k in (1, 2, 3):
            norms_z(k).start()

    def norms_next():
        for k in (1, 2, 3):
            norms_z(k).wait_recv()
        for k in (1, 2, 3):
            norms_y(k).start()

    def norms_last():
        for k in (1, 2, 3):
            norms_y(k).wait_recv()
        norms_core().start()
        norms_keep().start()

    events = []
    for unit in UNITS:
        b, p = unit
        first, rest = phases(unit)
        if unit in X_FIRST:
            when = X_WHEN[unit]
            last = when[-1]
            events += list(zip(when, first))
        else:
            for s in (0, 1):
                start = 8 * p + 4 * s + b
                when = [start, start + M_GAP, start + 2 * M_GAP, start + 3 * M_GAP, start + 4 * M_GAP]
                if start + M_GAP > 15:
                    when = [start] + [max(16, start) + n for n in range(4)]
                else:
                    when = [w if w <= 15 else 16 + n - [v <= 15 for v in when].count(True) for n, w in enumerate(when)]
                last = when[-1]
                events += list(zip(when, first[s]))
        for act in rest:
            last = last + REST_GAP if last + REST_GAP <= 15 else max(16, last + 1)
            events.append((last, act))
    end = max(when for when, act in events)
    norm_at = end - 1
    events += [(norm_at + n, act) for n, act in enumerate((norms_begin, norms_next, norms_last))]
    events = sorted(enumerate(events), key=lambda e: (e[1][0], e[0]))
    by_slot = {}
    for _, (when, act) in events:
        by_slot.setdefault(when, []).append(act)

    def step(s, _):
        @pl.when(s > 0)
        def _():
            amplitude_pairs(s, (0,))

        amplitude_pairs(s, (1, 2))
        amplitude_last(s)
        for b in range(4):
            compute(s, b)
            for k in range(4):
                acts = by_slot.get(4 * k + b, [])
                if acts:
                    @pl.when(s == k)
                    def _():
                        for act in acts:
                            act()
        return 0

    lax.fori_loop(0, 4, step, 0)
    for when in sorted(by_slot):
        if when > 15:
            for act in by_slot[when]:
                act()

    for unit in UNITS:
        core_copy(unit).wait_recv()
    norms_keep().wait()
    norms_core().wait_recv()

    def wait_exchange(i, _):
        exchange(i).wait_send()
        return 0

    lax.fori_loop(0, NC, wait_exchange, 0)
    for unit in UNITS:
        for way in (0, 1):
            for kind in range(3):
                if unit in X_FIRST:
                    x_put(unit, way, kind).wait_send()
                    x2_put(unit, way, kind).wait_send()
                else:
                    for s in (0, 1):
                        for slot in (0, 1):
                            m_put(unit, s, slot, way, kind).wait_send()
                        m2_put(unit, s, way, kind).wait_send()
        for k in (1, 2, 3):
            last_put(unit, k).wait_send()
            share(unit, k).wait_send()
            deliver(unit, k).wait_send()
        core_copy(unit).wait_send()
    for k in (1, 2, 3):
        norms_z(k).wait_send()
        norms_y(k).wait_send()
    norms_core().wait_send()


def ladders(plan, t2_window, factors):
    dma = pltpu.SemaphoreType.DMA
    any_space = pl.BlockSpec(memory_space=pl.ANY)
    smem = pl.BlockSpec(memory_space=pltpu.SMEM)
    vmem = pl.BlockSpec(memory_space=pltpu.VMEM)
    flops = 2 * FILLED * 8 * VT * VT * KC
    spread, norms, _ = pl.pallas_call(
        ladder_kernel,
        out_shape=(
            jax.ShapeDtypeStruct((2, 2, 16, VT, VT), BF),
            jax.ShapeDtypeStruct((2, 4, 4, 8, 128), F32),
            jax.ShapeDtypeStruct(factors.shape, BF),
        ),
        in_specs=[smem, vmem, any_space],
        out_specs=(any_space, any_space, any_space),
        scratch_shapes=[
            pltpu.VMEM((4, 512, 256), BF),
            pltpu.VMEM((53, 256, 256), BF),
            pltpu.VMEM((NC, VT, KC), BF),
            pltpu.VMEM((NC, KC, 256), BF),
            pltpu.VMEM((4, 2, FILLED, VT, VT), BF),
            pltpu.VMEM((2, 3, ROWS, W * VT), BF),
            pltpu.VMEM((8, 2, 3, 8, VT, VT), BF),
            pltpu.VMEM((8, 2, 3, 2, VT, VT), BF),
            pltpu.VMEM((8, 3, VT, VT), BF),
        ]
        + [pltpu.VMEM((4, VT, VT), BF) for _ in UNITS]
        + [
            pltpu.VMEM((2, 4, 4, 8, 128), F32),
            dma((NC,)), dma((NC,)), dma((2, 3)),
            dma((8, 2, 3, 4)), dma((8, 2, 3, 4)), dma((8, 2, 3, 2)), dma((8, 2, 3, 2)), dma((8, 3)), dma((8, 3)),
            dma((8, 3)), dma((8, 3)), dma((8, 3)), dma((8, 3)), dma((8,)), dma((8,)), dma((8,)),
            dma((3,)), dma((3,)), dma((3,)), dma((3,)), dma, dma, dma,
        ],
        compiler_params=pltpu.CompilerParams(
            collective_id=0, has_side_effects=True, vmem_limit_bytes=63 * 2**20
        ),
        cost_estimate=pl.CostEstimate(flops=flops, bytes_accessed=2**24, transcendentals=0),
    )(plan, t2_window, factors)
    return spread, norms


def home_kernel(plan, tiles, norms, residual, out, norms_out, wide):
    s = pl.program_id(0)
    for p in range(4):
        wide[p * 128:p * 128 + 128, :] = tiles[p // 2, p % 2, 0].astype(F32)
    keep = plan[4, s] == 1
    for a in range(VT):
        lanes = slice(a * 128, a * 128 + 128)
        ladder = wide[pl.ds(a, 4, stride=128), :]
        total = residual[0, :, lanes].astype(F32) + ladder
        out[0, :, lanes] = jnp.where(keep, total, 0.0).astype(BF)

    @pl.when(s == 0)
    def _():
        for i in range(2):
            for p in range(4):
                row = norms[pl.ds((p // 2) * 128 + plan[5, i] + p % 2, 1), :]
                norms_out[i, p] = jnp.max(row)


def at_home(plan, spread, norms, residual):
    return pl.pallas_call(
        home_kernel,
        out_shape=(
            jax.ShapeDtypeStruct(residual.shape, BF),
            jax.ShapeDtypeStruct((2, 4), F32),
        ),
        grid_spec=pltpu.PrefetchScalarGridSpec(
            num_scalar_prefetch=1,
            grid=(8,),
            in_specs=[
                pl.BlockSpec((2, 2, 1, VT, VT), lambda s, plan: (0, 0, plan[3, s], 0, 0)),
                pl.BlockSpec((256, 128), lambda s, plan: (0, 0)),
                pl.BlockSpec((1, 4, VT * VT), lambda s, plan: (s, 0, 0)),
            ],
            out_specs=[
                pl.BlockSpec((1, 4, VT * VT), lambda s, plan: (s, 0, 0)),
                pl.BlockSpec(memory_space=pltpu.SMEM),
            ],
            scratch_shapes=[pltpu.VMEM((4 * VT, VT), F32)],
        ),
    )(plan, spread, norms.reshape(256, 128), residual)


def plan_kernel(tile_mask, owner_slot, home_slot, plan):
    x, y, z, c = place()
    w = lax.axis_index("wide")
    n = 256
    r = lax.broadcasted_iota(I32, (n, n), 0)
    l = lax.broadcasted_iota(I32, (n, n), 1)
    eye = r == l

    def column(v):
        return jnp.sum(jnp.where(eye, v, 0), axis=1, keepdims=True)

    def pick(mask, v):
        return jnp.sum(jnp.where(mask, v, 0), axis=0, keepdims=True)

    mask_row, owner_row, home_row = tile_mask[...], owner_slot[...], home_slot[...]
    filled, home, owner = column(mask_row) == 1, column(home_row), column(owner_row)
    before = (mask_row == 1) & (home_row < home)
    where = jnp.sum(jnp.where(before, 1, 0), axis=1, keepdims=True)
    cell, turn = where & 15, where >> 4
    index = cell * 4 + turn
    match = filled & (index == l)
    ids = lax.broadcasted_iota(I32, (n, 1), 0)
    first_of = (ids * 4370) >> 16
    plan[0:1, :] = pick(match, first_of)
    plan[1:2, :] = pick(match, ids - first_of * NC)
    chips = pick(match, home >> 4)
    r16 = lax.broadcasted_iota(I32, (16, n), 0)
    t16 = lax.broadcasted_iota(I32, (16, n), 1)
    batch, k = r16 >> 2, r16 & 3
    by_y = (batch & 1) == 0
    group = jnp.where(by_y, y, z)
    far = (group + k) & 3
    target = jnp.where(by_y, z * 4 + far, far * 4 + y)
    hit = (t16 < FILLED) & ((t16 >> 4) == batch) & (((t16 >> 2) & 3) == group) & (chips == target)
    choice = jnp.sum(jnp.where(hit, t16 & 3, 0), axis=1, keepdims=True)
    plan[2:3, :] = pick(r16 == t16, choice)
    here = filled & (home == w * 8 + l) & (l < 8)
    plan[3:4, :] = pick(here, cell)
    plan[4:5, :] = pick(here, 1)
    batch_of, group_of = cell >> 2, cell & 3
    chip_of = jnp.where((batch_of & 1) == 0, turn * 4 + group_of, group_of * 4 + turn)
    plan[5:6, :] = pick(filled & (owner == w * 2 + l) & (l < 2), chip_of * 8 + 2 * batch_of)
    plan[6:8, :] = jnp.zeros((2, n), I32)


def make_plan(tile_mask, owner_slot, home_slot):
    rows = [jnp.pad(v, (0, 256 - NT)).reshape(1, 256) for v in (tile_mask, owner_slot, home_slot)]
    return pl.pallas_call(plan_kernel, out_shape=jax.ShapeDtypeStruct((8, 256), I32))(*rows)


def body(factors, t2_window, residual_in, tile_mask, owner_slot, home_slot):
    plan = make_plan(tile_mask, owner_slot, home_slot)
    spread, norms = ladders(plan, t2_window, factors)
    return at_home(plan, spread, norms, residual_in)


def solution(mesh):
    in_specs = (P(None, ("wide", "narrow"), None), P(), P("wide", "narrow", None), P(), P(), P())
    out_specs = (P("wide", "narrow", None), P("wide", "narrow"))
    return jax.shard_map(body, mesh=mesh, in_specs=in_specs, out_specs=out_specs, check_vma=False)
```

time: 744 us -> 167 us (0.22)
  waiting for transfers between devices: 416 us -> 0 us
  Pallas kernels: 0 us -> 160 us
  local copies, waits for them, and re-layouts: 121 us -> 5.21 us
  matrix products: 95.4 us -> 0 us
  loops' own time: 29.6 us -> 0 us
  blocking collectives: 29.3 us -> 0 us
  other arithmetic: 22 us -> 0 us
  between operations: 15.1 us -> 0.76 us
  starting transfers between devices: 9.84 us -> 0 us
    all_to_all x1 -> x0, waiting for transfers between devices: 336 us -> none  [body(): lax.all_to_all(outgoing, 'wide', split_axis=0, concat_axis=0, tiled=True)]
    pallas_call x0 -> x3, Pallas kernels: none -> 160 us  [the longest x1 152 us: ladders(): pl.pallas_call(ladder_kernel, out_shape=(jax.ShapeDtypeStruct((2, 2, 16,...]
    dot_general x5 -> x0, matrix products: 95.4 us -> none  [the longest x2 41.2 us: tile_contract(): lax.dot_general(first_side, second_side, (((0,), (0,)), ((), ())), prefer...]
    all_gather x1 -> x0, waiting for transfers between devices: 79.8 us -> none  [body(): gathered_rows = lax.all_gather(ladder, 'wide', axis=0, tiled=True)]
    dot_general x6 -> x0, local copies, waits for them, and re-layouts: 40.2 us -> none  [the longest x4 39.6 us: tile_contract(): lax.dot_general(first_side, second_side, (((0,), (0,)), ((), ())), prefer...]
    dynamic_update_slice x2 -> x0, local copies, waits for them, and re-layouts: 37 us -> none  [body(): lax.map(one_tile, jnp.arange(received.shape[1], dtype=jnp.int32))]
    another operation x1 -> x0, loops' own time: 29.6 us -> none  [body(): lax.map(one_tile, jnp.arange(received.shape[1], dtype=jnp.int32))]
    unnamed x1 -> x0, blocking collectives: 29.3 us -> none
  transfers between devices with their start and end apart: 2 -> 0, of which waited for: 2 -> 0; matrix products, arithmetic and copies ran while one was open for 0% -> 0% of each run, Pallas kernels for 0% -> 0%
where the time goes in v3:
time: 167 us; the launch traced here: 166 us
  Pallas kernels  160 us (96%)
  local copies, waits for them, and re-layouts  5.21 us (3%)
    pallas_call x1, Pallas kernels, ladders(): pl.pallas_call(ladder_kernel, out_shape=(jax.ShapeDtypeStruct((2, 2, 16,...  152 us
    pallas_call x1, Pallas kernels, at_home(): pl.pallas_call(home_kernel, out_shape=(jax.ShapeDtypeStruct(residual.shap...  7.14 us
    pad x3, local copies, waits for them, and re-layouts, make_plan(): jnp.pad(v, (0, 256 - NT)).reshape(1, 256)  3.74 us

profile of v3, /device:TPU:1, one launch (start us, length us, event | category | flops | bytes accessed | tf_op | source)
XLA Modules:
  0.0 166.5 jit_solution(4546052250126435148)
XLA Ops:
  0.6 1.2 pad.10
  1.9 1.2 pad.11
  3.1 1.3 pad.12
  4.4 1.8 %shard_map.77.plan = s32[8,256]{1,0:T(8,128)} custom-call(s32[1,256]{1,0:T(1,128)} %bitcast.5, s32[1,256]{1,0:T(1,128)} %bitcast.6, s32[1,256]{1,0:T(1,128)} %bitcast.7), custom_call_target="tpu_custom_call" | custom-call | tf_op jit(solution)/shard_map/pallas_call | solution.py:674
  6.2 1.5 copy.8.t2
  7.7 151.5 %shard_map.78 = (bf16[2,2,16,128,128]{4,3,2,1,0:T(8,128)(2,1)}, f32[2,4,4,8,128]{4,3,2,1,0:T(8,128)}, bf16[15,56,1920]{2,1,0:T(8,128)(2,1)}) custom-call(s32[8,256]{1,0:T(8,128)} %shard_map.77.plan, bf16[16,15,15]{2,1,0:T(8,128)(2,1)} %copy.8.t2, bf16[15,56,1920]{2,1,0:T(8,128)(2,1)} %own_rows.1), custom_call_target="tpu_custom_call" | custom-call | flops 30064771072 | bytes 16777216 | tf_op jit(solution)/shard_map/pallas_call | solution.py:548
  159.2 7.1 %shard_map.79 = (bf16[8,4,16384]{2,1,0:T(4,128)(2,1)}, f32[2,4]{1,0:T(2,128)}) custom-call(s32[8,256]{1,0:T(8,128)} %shard_map.77.plan, bf16[2,2,16,128,128]{4,3,2,1,0:T(8,128)(2,1)} %get-tuple-element.4.tiles, f32[256,128]{1,0:T(8,128)} %bitcast.4, bf16[8,4,16384]{2,1,0:T(4,128)(2,1)} %residual.1), custom_call_target="tpu_custom_call" | custom-call | tf_op jit(solution)/shard_map/pallas_call | solution.py:604

commit v4 on v3

--- a/solution.py
+++ b/solution.py
@@ -25,10 +25,10 @@
 
 
 X_WHEN = {
-    (0, 0): (0, 4, 11, 12, 13),
-    (1, 0): (1, 5, 12, 13, 14),
-    (0, 1): (8, 12, 17, 18, 19),
-    (1, 1): (9, 13, 17, 18, 19),
+    (0, 0): (0, 4, 11, 13),
+    (1, 0): (1, 5, 12, 14),
+    (0, 1): (8, 12, 17, 18),
+    (1, 1): (9, 13, 17, 18),
 }
 M_GAP = 2
 REST_GAP = 1
@@ -235,35 +235,25 @@
                 x_put(unit, way, kind).wait_recv()
         for half in range(2):
             add_tiles(x_part(unit, 0, half), [r1.at[u, half, 2], r1.at[u, 1 - half, 1]], 8)
-        for kind in (0, 1):
-            for way in (0, 1):
-                x2_put(unit, way, kind).start()
-
-    def x2_part(unit, k, half):
+        for k in (2, 1, 3):
+            x2_put(unit, k).start()
+
+    def x2_part(unit, k):
         b, p = unit
         base, hi, lo = corner(b)
-        return out.at[2 * p + 1, 1, pl.ds(base + ((hi + k) % 4) * 4 + 2 * half, 2)]
-
-    def x2_put(unit, way, kind):
+        return out.at[2 * p + 1, 1, pl.ds(base + ((hi + k) % 4) * 4, 4)]
+
+    def x2_put(unit, k):
         u = number(unit)
         return remote(
-            x2_part(unit, *route(way, kind)), r2.at[u, way, kind], s2_s.at[u, way, kind, 0],
-            s2_r.at[u, way, kind, 0], ring[MAJOR[unit[0]]][1][3 if way else 1],
+            x2_part(unit, k), r2.at[u, k - 1], s2_s.at[u, k - 1, 0], s2_r.at[u, k - 1, 0], ring[MAJOR[unit[0]]][1][k]
         )
 
-    def x2_pass(unit):
-        for way in (0, 1):
-            x2_put(unit, way, 0).wait_recv()
-            add_tiles(x2_part(unit, *route(way, 2)), [r2.at[number(unit), way, 0]], 2)
-            x2_put(unit, way, 2).start()
-
     def x2_sum(unit):
         u = number(unit)
-        for way in (0, 1):
-            for kind in (1, 2):
-                x2_put(unit, way, kind).wait_recv()
-        for half in range(2):
-            add_tiles(x2_part(unit, 0, half), [r2.at[u, half, 2], r2.at[u, 1 - half, 1]], 2)
+        for k in (1, 2, 3):
+            x2_put(unit, k).wait_recv()
+        add_tiles(x2_part(unit, 0), [r2.at[u, k] for k in range(3)], 4)
         last_send(unit)
 
     def m_part(unit, s, k, half):
@@ -309,38 +299,26 @@
                     m_part(unit, s, 0, half).at[slot],
                     [m_land(unit, s, half, 2).at[two], m_land(unit, s, 1 - half, 1).at[two]], 2,
                 )
-        for kind in (0, 1):
-            for way in (0, 1):
-                m2_put(unit, s, way, kind).start()
-
-    def m2_part(unit, s, k, half):
+        for k in (2, 1, 3):
+            m2_put(unit, s, k).start()
+
+    def m2_part(unit, s, k):
         b, p = unit
         base, hi, lo = corner(b)
-        return out.at[2 * p + s, half, base + hi * 4 + (lo + k) % 4]
-
-    def m2_put(unit, s, way, kind):
+        return out.at[2 * p + s, :, base + hi * 4 + (lo + k) % 4]
+
+    def m2_put(unit, s, k):
         u = number(unit)
         return remote(
-            m2_part(unit, s, *route(way, kind)), r2.at[u, way, kind, s], s2_s.at[u, way, kind, s],
-            s2_r.at[u, way, kind, s], ring[MINOR[unit[0]]][1][3 if way else 1],
+            m2_part(unit, s, k), r2.at[u, k - 1, 2 * s:2 * s + 2], s2_s.at[u, k - 1, s], s2_r.at[u, k - 1, s],
+            ring[MINOR[unit[0]]][1][k],
         )
 
-    def m2_pass(unit, s):
-        for way in (0, 1):
-            m2_put(unit, s, way, 0).wait_recv()
-            dst = m2_part(unit, s, *route(way, 2))
-            dst[...] = (dst[...].astype(F32) + r2[number(unit), way, 0, s].astype(F32)).astype(BF)
-            m2_put(unit, s, way, 2).start()
-
     def m2_sum(unit, s):
         u = number(unit)
-        for way in (0, 1):
-            for kind in (1, 2):
-                m2_put(unit, s, way, kind).wait_recv()
-        for half in range(2):
-            dst = m2_part(unit, s, 0, half)
-            total = dst[...].astype(F32) + r2[u, half, 2, s].astype(F32) + r2[u, 1 - half, 1, s].astype(F32)
-            dst[...] = total.astype(BF)
+        for k in (1, 2, 3):
+            m2_put(unit, s, k).wait_recv()
+        add_tiles(m2_part(unit, s, 0), [r2.at[u, k, 2 * s:2 * s + 2] for k in range(3)], 2)
         if s == 1:
             last_send(unit)
 
@@ -418,9 +396,9 @@
     def phases(unit):
         bind = functools.partial
         if unit in X_FIRST:
-            first = [bind(f, unit) for f in (x_begin, x_pass, x_sum, x2_pass, x2_sum)]
+            first = [bind(f, unit) for f in (x_begin, x_pass, x_sum, x2_sum)]
         else:
-            acts = (m_begin, m_pass, m_sum, m2_pass, m2_sum)
+            acts = (m_begin, m_pass, m_sum, m2_sum)
             first = [[bind(f, unit, s) for f in acts] for s in (0, 1)]
         return first, [bind(f, unit) for f in (last_sum, handout, finish)]
 
@@ -465,9 +443,9 @@
         else:
             for s in (0, 1):
                 start = 8 * p + 4 * s + b
-                when = [start, start + M_GAP, start + 2 * M_GAP, start + 3 * M_GAP, start + 4 * M_GAP]
+                when = [start + n * M_GAP for n in range(4)]
                 if start + M_GAP > 15:
-                    when = [start] + [max(16, start) + n for n in range(4)]
+                    when = [start] + [max(16, start) + n for n in range(3)]
                 else:
                     when = [w if w <= 15 else 16 + n - [v <= 15 for v in when].count(True) for n, w in enumerate(when)]
                 last = when[-1]
@@ -476,7 +454,7 @@
             last = last + REST_GAP if last + REST_GAP <= 15 else max(16, last + 1)
             events.append((last, act))
     end = max(when for when, act in events)
-    norm_at = end - 1
+    norm_at = end - 2
     events += [(norm_at + n, act) for n, act in enumerate((norms_begin, norms_next, norms_last))]
     events = sorted(enumerate(events), key=lambda e: (e[1][0], e[0]))
     by_slot = {}
@@ -522,13 +500,16 @@
             for kind in range(3):
                 if unit in X_FIRST:
                     x_put(unit, way, kind).wait_send()
-                    x2_put(unit, way, kind).wait_send()
                 else:
                     for s in (0, 1):
                         for slot in (0, 1):
                             m_put(unit, s, slot, way, kind).wait_send()
-                        m2_put(unit, s, way, kind).wait_send()
-        for k in (1, 2, 3):
+        for k in (1, 2, 3):
+            if unit in X_FIRST:
+                x2_put(unit, k).wait_send()
+            else:
+                for s in (0, 1):
+                    m2_put(unit, s, k).wait_send()
             last_put(unit, k).wait_send()
             share(unit, k).wait_send()
             deliver(unit, k).wait_send()
@@ -562,14 +543,14 @@
             pltpu.VMEM((4, 2, FILLED, VT, VT), BF),
             pltpu.VMEM((2, 3, ROWS, W * VT), BF),
             pltpu.VMEM((8, 2, 3, 8, VT, VT), BF),
-            pltpu.VMEM((8, 2, 3, 2, VT, VT), BF),
+            pltpu.VMEM((8, 3, 4, VT, VT), BF),
             pltpu.VMEM((8, 3, VT, VT), BF),
         ]
         + [pltpu.VMEM((4, VT, VT), BF) for _ in UNITS]
         + [
             pltpu.VMEM((2, 4, 4, 8, 128), F32),
             dma((NC,)), dma((NC,)), dma((2, 3)),
-            dma((8, 2, 3, 4)), dma((8, 2, 3, 4)), dma((8, 2, 3, 2)), dma((8, 2, 3, 2)), dma((8, 3)), dma((8, 3)),
+            dma((8, 2, 3, 4)), dma((8, 2, 3, 4)), dma((8, 3, 2)), dma((8, 3, 2)), dma((8, 3)), dma((8, 3)),
             dma((8, 3)), dma((8, 3)), dma((8, 3)), dma((8, 3)), dma((8,)), dma((8,)), dma((8,)),
             dma((3,)), dma((3,)), dma((3,)), dma((3,)), dma, dma, dma,
         ],
@@ -624,7 +605,7 @@
     )(plan, spread, norms.reshape(256, 128), residual)
 
 
-def plan_kernel(tile_mask, owner_slot, home_slot, plan):
+def plan_kernel(rows, plan):
     x, y, z, c = place()
     w = lax.axis_index("wide")
     n = 256
@@ -638,7 +619,7 @@
     def pick(mask, v):
         return jnp.sum(jnp.where(mask, v, 0), axis=0, keepdims=True)
 
-    mask_row, owner_row, home_row = tile_mask[...], owner_slot[...], home_slot[...]
+    mask_row, owner_row, home_row = rows[0:1, :], rows[1:2, :], rows[2:3, :]
     filled, home, owner = column(mask_row) == 1, column(home_row), column(owner_row)
     before = (mask_row == 1) & (home_row < home)
     where = jnp.sum(jnp.where(before, 1, 0), axis=1, keepdims=True)
@@ -670,8 +651,8 @@
 
 
 def make_plan(tile_mask, owner_slot, home_slot):
-    rows = [jnp.pad(v, (0, 256 - NT)).reshape(1, 256) for v in (tile_mask, owner_slot, home_slot)]
-    return pl.pallas_call(plan_kernel, out_shape=jax.ShapeDtypeStruct((8, 256), I32))(*rows)
+    rows = jnp.pad(jnp.stack([tile_mask, owner_slot, home_slot]), ((0, 5), (0, 256 - NT)))
+    return pl.pallas_call(plan_kernel, out_shape=jax.ShapeDtypeStruct((8, 256), I32))(rows)
 
 
 def body(factors, t2_window, residual_in, tile_mask, owner_slot, home_slot):

time: 167 us -> 157 us (0.940)
  Pallas kernels: 160 us -> 152 us
  local copies, waits for them, and re-layouts: 5.21 us -> 2.08 us
    pallas_call x1, Pallas kernels: 152 us -> 144 us  [ladders(): pl.pallas_call(ladder_kernel, out_shape=(jax.ShapeDtypeStruct((2, 2, 16,...]
    pad x3 -> x1, local copies, waits for them, and re-layouts: 3.74 us -> 0.6 us  [make_plan(): jnp.pad(jnp.stack([tile_mask, owner_slot, home_slot]), ((0, 5), (0, 256 -...]
where the time goes in v4:
time: 157 us; the launch traced here: 156 us
  Pallas kernels  152 us (97%)
  local copies, waits for them, and re-layouts  2.08 us (1%)
    pallas_call x1, Pallas kernels, ladders(): pl.pallas_call(ladder_kernel, out_shape=(jax.ShapeDtypeStruct((2, 2, 16,...  144 us
    pallas_call x1, Pallas kernels, at_home(): pl.pallas_call(home_kernel, out_shape=(jax.ShapeDtypeStruct(residual.shap...  7.13 us

profile of v4, /device:TPU:1, one launch (start us, length us, event | category | flops | bytes accessed | tf_op | source)
XLA Modules:
  0.0 156.0 jit_solution(2760676925532187073)
XLA Ops:
  0.6 0.7 pad_add_fusion
  1.4 0.6 pad.4.rows
  2.0 1.8 %shard_map.77.plan = s32[8,256]{1,0:T(8,128)} custom-call(s32[8,256]{1,0:T(8,128)} %pad.4.rows), custom_call_target="tpu_custom_call" | custom-call | tf_op jit(solution)/shard_map/pallas_call | solution.py:655
  3.8 1.5 copy.8.t2
  5.3 143.5 %shard_map.78 = (bf16[2,2,16,128,128]{4,3,2,1,0:T(8,128)(2,1)}, f32[2,4,4,8,128]{4,3,2,1,0:T(8,128)}, bf16[15,56,1920]{2,1,0:T(8,128)(2,1)}) custom-call(s32[8,256]{1,0:T(8,128)} %shard_map.77.plan, bf16[16,15,15]{2,1,0:T(8,128)(2,1)} %copy.8.t2, bf16[15,56,1920]{2,1,0:T(8,128)(2,1)} %own_rows.1), custom_call_target="tpu_custom_call" | custom-call | flops 30064771072 | bytes 16777216 | tf_op jit(solution)/shard_map/pallas_call | solution.py:529
  148.8 7.1 %shard_map.79 = (bf16[8,4,16384]{2,1,0:T(4,128)(2,1)}, f32[2,4]{1,0:T(2,128)}) custom-call(s32[8,256]{1,0:T(8,128)} %shard_map.77.plan, bf16[2,2,16,128,128]{4,3,2,1,0:T(8,128)(2,1)} %get-tuple-element.4.tiles, f32[256,128]{1,0:T(8,128)} %bitcast.4, bf16[8,4,16384]{2,1,0:T(4,128)(2,1)} %residual.1), custom_call_target="tpu_custom_call" | custom-call | tf_op jit(solution)/shard_map/pallas_call | solution.py:585

commit v5 on v4

--- a/solution.py
+++ b/solution.py
@@ -24,12 +24,7 @@
 X_FIRST = {(0, 0), (1, 0), (0, 1), (1, 1)}
 
 
-X_WHEN = {
-    (0, 0): (0, 4, 11, 13),
-    (1, 0): (1, 5, 12, 14),
-    (0, 1): (8, 12, 17, 18),
-    (1, 1): (9, 13, 17, 18),
-}
+X_WHEN = {(0, 0): (0, 4, 10, 12), (1, 0): (1, 5, 11, 13), (0, 1): (8, 12, 17, 18), (1, 1): (9, 13, 17, 18)}
 M_GAP = 2
 REST_GAP = 1
 

time: 157 us -> 155 us (0.987)
    pallas_call x1, Pallas kernels: 144 us -> 142 us  [ladders(): pl.pallas_call(ladder_kernel, out_shape=(jax.ShapeDtypeStruct((2, 2, 16,...]
where the time goes in v5:
time: 155 us; the launch traced here: 154 us
  Pallas kernels  151 us (97%)
  local copies, waits for them, and re-layouts  2.08 us (1%)
    pallas_call x1, Pallas kernels, ladders(): pl.pallas_call(ladder_kernel, out_shape=(jax.ShapeDtypeStruct((2, 2, 16,...  142 us
    pallas_call x1, Pallas kernels, at_home(): pl.pallas_call(home_kernel, out_shape=(jax.ShapeDtypeStruct(residual.shap...  7.07 us

profile of v5, /device:TPU:1, one launch (start us, length us, event | category | flops | bytes accessed | tf_op | source)
XLA Modules:
  0.0 154.2 jit_solution(4960876195312116134)
XLA Ops:
  0.6 0.7 pad_add_fusion
  1.4 0.6 pad.4.rows
  2.0 1.8 %shard_map.77.plan = s32[8,256]{1,0:T(8,128)} custom-call(s32[8,256]{1,0:T(8,128)} %pad.4.rows), custom_call_target="tpu_custom_call" | custom-call | tf_op jit(solution)/shard_map/pallas_call | solution.py:650
  3.8 1.5 copy.8.t2
  5.3 141.8 %shard_map.78 = (bf16[2,2,16,128,128]{4,3,2,1,0:T(8,128)(2,1)}, f32[2,4,4,8,128]{4,3,2,1,0:T(8,128)}, bf16[15,56,1920]{2,1,0:T(8,128)(2,1)}) custom-call(s32[8,256]{1,0:T(8,128)} %shard_map.77.plan, bf16[16,15,15]{2,1,0:T(8,128)(2,1)} %copy.8.t2, bf16[15,56,1920]{2,1,0:T(8,128)(2,1)} %own_rows.1), custom_call_target="tpu_custom_call" | custom-call | flops 30064771072 | bytes 16777216 | tf_op jit(solution)/shard_map/pallas_call | solution.py:524
  147.0 7.1 %shard_map.79 = (bf16[8,4,16384]{2,1,0:T(4,128)(2,1)}, f32[2,4]{1,0:T(2,128)}) custom-call(s32[8,256]{1,0:T(8,128)} %shard_map.77.plan, bf16[2,2,16,128,128]{4,3,2,1,0:T(8,128)(2,1)} %get-tuple-element.4.tiles, f32[256,128]{1,0:T(8,128)} %bitcast.4, bf16[8,4,16384]{2,1,0:T(4,128)(2,1)} %residual.1), custom_call_target="tpu_custom_call" | custom-call | tf_op jit(solution)/shard_map/pallas_call | solution.py:580
